TPU v7x, 32 devices: a whole 2x2x4 slice. The times are simulated.
32 devices in a mesh: dp: 16 (over z, x, core), band: 2 (over y).
Axes of the slice: x: 2, y: 2, z: 4, core: 2. Of those that a mesh axis runs over, the one named last changes fastest.
Arguments:
- pixels: bfloat16 [384, 10, 256, 64], P('dp', 'band'), may hold values from -6 to 6
- visible: int32 [384, 64], P('dp'), may hold values from 0 to 255, as said below
- kernels: bfloat16 [10, 64, 768], P('band'), may hold values from -0.25 to 0.25
- class_token: float32 [768], replicated, may hold values from -5 to 5
- norm1_gain: float32 [768], replicated, may hold values from 0.1 to 1.9
- norm1_bias: float32 [768], replicated, may hold values from -3 to 3
- norm2_gain: float32 [768], replicated, may hold values from 0.1 to 1.9
- norm2_bias: float32 [768], replicated, may hold values from -3 to 3
- attn_qkv: bfloat16 [768, 2304], replicated, may hold values from -0.21875 to 0.21875
- attn_out: bfloat16 [768, 768], replicated, may hold values from -0.4375 to 0.4375
- mlp_up: bfloat16 [768, 3072], replicated, may hold values from -0.21875 to 0.21875
- mlp_down: bfloat16 [3072, 768], replicated, may hold values from -0.109375 to 0.109375
- cotangent: bfloat16 [384, 65, 768], P(('dp', 'band')), may hold values from -6 to 6
Outputs:
- block_output: bfloat16 [384, 65, 768], P(('dp', 'band'))
- pixel_grads: float32 [384, 10, 256, 64], P('dp', 'band')
- kernel_grads: float32 [10, 64, 768], P('band')
- class_grad: float32 [768], replicated
- norm1_gain_grad: float32 [768], replicated
- norm1_bias_grad: float32 [768], replicated
- norm2_gain_grad: float32 [768], replicated
- norm2_bias_grad: float32 [768], replicated
- qkv_grad: float32 [768, 2304], P('band', 'dp')
- outproj_grad: float32 [768, 768], P('band', 'dp')
- up_grad: float32 [768, 3072], P('band', 'dp')
- down_grad: float32 [3072, 768], P('band', 'dp')
Inputs may be any that keep to these rules, and one draw needn't show every extreme that they name: `visible`: each row holds 64 different patch numbers, in no particular order.
All inputs are finite; a program needn't handle non-finite values.
Results may differ from a plain program's by a relative error of at most 0.015.
Values may be sent and summed in bfloat16 or wider, within the bound.
No kernel may reach another device: no remote copies, remote signals or barrier semaphores. Data moves between devices by JAX's collectives and lax.ppermute only.
A program may use at most 192 MiB of HBM per device.

v0:
```python
import jax
import jax.numpy as jnp
from jax import lax
from jax.sharding import PartitionSpec as P

HEADS = 12
HEAD = 64


def layer_norm(values, norm_gain, norm_bias):
    average = jnp.mean(values, axis=-1, keepdims=True)
    centred = values - average
    spread = jnp.mean(centred * centred, axis=-1, keepdims=True)
    return centred * lax.rsqrt(spread + 1e-06) * norm_gain + norm_bias


def gelu_exact(values):
    return jax.nn.gelu(values, approximate=False)


def shards(
    pixels,
    visible,
    kernels,
    class_token,
    norm1_gain,
    norm1_bias,
    norm2_gain,
    norm2_bias,
    attn_qkv,
    attn_out,
    mlp_up,
    mlp_down,
    cotangent,
):
    model_width = attn_out.shape[0]
    head_count = HEADS
    head_size = HEAD
    local_chips = cotangent.shape[0]
    seq_tokens = cotangent.shape[1]
    total_rows = local_chips * seq_tokens
    scaling = head_size ** (-0.5)
    patch_total = pixels.shape[2]
    patch_ids = lax.broadcasted_iota(jnp.int32, (1, 1, patch_total), 2)
    selector = visible[:, :, None] == patch_ids
    selector_low = selector.astype(jnp.bfloat16)
    picked = jnp.einsum(
        "cvn,cbnp->cbvp", selector_low, pixels, preferred_element_type=jnp.float32
    ).astype(jnp.bfloat16)
    embedded = lax.psum_scatter(
        jnp.einsum("cbvp,bpd->cvd", picked, kernels, preferred_element_type=jnp.float32),
        "band",
        scatter_dimension=0,
        tiled=True,
    )
    leading = jnp.broadcast_to(class_token[None, None, :], (local_chips, 1, model_width))
    stream = jnp.concatenate([leading, embedded], axis=1).reshape(total_rows, model_width)
    normed1_low = layer_norm(stream, norm1_gain, norm1_bias).astype(jnp.bfloat16)
    packed = jnp.dot(normed1_low, attn_qkv, preferred_element_type=jnp.float32).astype(jnp.bfloat16)
    packed = packed.reshape(local_chips, seq_tokens, 3, head_count, head_size)
    queries = packed[:, :, 0]
    keys_all = packed[:, :, 1]
    values_all = packed[:, :, 2]
    scores = (
        jnp.einsum("cqhe,ckhe->chqk", queries, keys_all, preferred_element_type=jnp.float32)
        * scaling
    )
    row_max = jnp.max(scores, axis=-1, keepdims=True)
    raised = jnp.exp(scores - row_max)
    row_total = jnp.sum(raised, axis=-1, keepdims=True)
    probs_low = (raised / row_total).astype(jnp.bfloat16)
    log_total = row_max + jnp.log(row_total)
    attended = jnp.einsum(
        "chqk,ckhe->cqhe", probs_low, values_all, preferred_element_type=jnp.float32
    )
    attended_low = attended.astype(jnp.bfloat16).reshape(total_rows, model_width)
    mid_stream = stream + jnp.dot(attended_low, attn_out, preferred_element_type=jnp.float32)
    normed2_low = layer_norm(mid_stream, norm2_gain, norm2_bias).astype(jnp.bfloat16)
    hidden_pre = jnp.dot(normed2_low, mlp_up, preferred_element_type=jnp.float32)
    activated_low = gelu_exact(hidden_pre).astype(jnp.bfloat16)
    result_rows = mid_stream + jnp.dot(activated_low, mlp_down, preferred_element_type=jnp.float32)
    block_output = result_rows.astype(jnp.bfloat16).reshape(local_chips, seq_tokens, model_width)
    grad_out = cotangent.reshape(total_rows, model_width)
    grad_down = jnp.einsum("rf,rd->fd", activated_low, grad_out, preferred_element_type=jnp.float32)
    grad_act = jnp.einsum("rd,fd->rf", grad_out, mlp_down, preferred_element_type=jnp.float32)
    unused_gelu, gelu_back = jax.vjp(gelu_exact, hidden_pre)
    grad_pre_low = gelu_back(grad_act)[0].astype(jnp.bfloat16)
    grad_up = jnp.einsum("rd,rf->df", normed2_low, grad_pre_low, preferred_element_type=jnp.float32)
    grad_normed2 = jnp.einsum("rf,df->rd", grad_pre_low, mlp_up, preferred_element_type=jnp.float32)
    unused_norm2, norm2_back = jax.vjp(layer_norm, mid_stream, norm2_gain, norm2_bias)
    grad_mid_norm, grad_gain2, grad_bias2 = norm2_back(grad_normed2)
    grad_mid = grad_out.astype(jnp.float32) + grad_mid_norm
    grad_branch_low = grad_mid.astype(jnp.bfloat16)
    grad_outproj = jnp.einsum(
        "rd,re->de", attended_low, grad_branch_low, preferred_element_type=jnp.float32
    )
    grad_attended = jnp.einsum(
        "re,de->rd", grad_branch_low, attn_out, preferred_element_type=jnp.float32
    )
    grad_attended = grad_attended.astype(jnp.bfloat16).reshape(
        local_chips, seq_tokens, head_count, head_size
    )
    grad_values = jnp.einsum(
        "chqk,cqhe->ckhe", probs_low, grad_attended, preferred_element_type=jnp.float32
    )
    grad_probs = jnp.einsum(
        "cqhe,ckhe->chqk", grad_attended, values_all, preferred_element_type=jnp.float32
    )
    again = (
        jnp.einsum("cqhe,ckhe->chqk", queries, keys_all, preferred_element_type=jnp.float32)
        * scaling
    )
    probs_again = jnp.exp(again - log_total)
    inner = jnp.sum(grad_probs * probs_again, axis=-1, keepdims=True)
    grad_scores_low = (probs_again * (grad_probs - inner) * scaling).astype(jnp.bfloat16)
    grad_queries = jnp.einsum(
        "chqk,ckhe->cqhe", grad_scores_low, keys_all, preferred_element_type=jnp.float32
    )
    grad_keys = jnp.einsum(
        "chqk,cqhe->ckhe", grad_scores_low, queries, preferred_element_type=jnp.float32
    )
    grad_packed = jnp.stack([grad_queries, grad_keys, grad_values], axis=2).astype(jnp.bfloat16)
    grad_packed = grad_packed.reshape(total_rows, 3 * model_width)
    grad_qkv = jnp.einsum("rd,re->de", normed1_low, grad_packed, preferred_element_type=jnp.float32)
    grad_normed1 = jnp.einsum(
        "re,de->rd", grad_packed, attn_qkv, preferred_element_type=jnp.float32
    )
    unused_norm1, norm1_back = jax.vjp(layer_norm, stream, norm1_gain, norm1_bias)
    grad_stream_norm, grad_gain1, grad_bias1 = norm1_back(grad_normed1)
    grad_stream = (grad_mid + grad_stream_norm).reshape(local_chips, seq_tokens, model_width)
    grad_class = jnp.sum(grad_stream[:, 0, :], axis=0)
    grad_embed_low = grad_stream[:, 1:, :].astype(jnp.bfloat16)
    group_grads = lax.all_gather(grad_embed_low, "band", axis=0, tiled=True)
    kernel_part = jnp.einsum(
        "cbvp,cvd->bpd", picked, group_grads, preferred_element_type=jnp.float32
    )
    spread_grads = jnp.einsum(
        "cvn,cvd->cnd", selector_low, group_grads, preferred_element_type=jnp.float32
    ).astype(jnp.bfloat16)
    pixel_grads = jnp.einsum(
        "cnd,bpd->cbnp", spread_grads, kernels, preferred_element_type=jnp.float32
    )
    kernel_grads = lax.psum(kernel_part, "dp")
    qkv_part, outproj_part, up_part, down_part = (
        lax.psum_scatter(
            grad_qkv.astype(jnp.bfloat16), "band", scatter_dimension=0, tiled=True
        ).astype(jnp.float32),
        lax.psum_scatter(
            grad_outproj.astype(jnp.bfloat16), "band", scatter_dimension=0, tiled=True
        ).astype(jnp.float32),
        lax.psum_scatter(
            grad_up.astype(jnp.bfloat16), "band", scatter_dimension=0, tiled=True
        ).astype(jnp.float32),
        lax.psum_scatter(
            grad_down.astype(jnp.bfloat16), "band", scatter_dimension=0, tiled=True
        ).astype(jnp.float32),
    )
    qkv_final, outproj_final, up_final, down_final = (
        lax.psum_scatter(qkv_part, "dp", scatter_dimension=1, tiled=True),
        lax.psum_scatter(outproj_part, "dp", scatter_dimension=1, tiled=True),
        lax.psum_scatter(up_part, "dp", scatter_dimension=1, tiled=True),
        lax.psum_scatter(down_part, "dp", scatter_dimension=1, tiled=True),
    )
    gain1_total, bias1_total, gain2_total, bias2_total, class_total = lax.psum(
        (grad_gain1, grad_bias1, grad_gain2, grad_bias2, grad_class), ("dp", "band")
    )
    return (
        block_output,
        pixel_grads,
        kernel_grads,
        class_total,
        gain1_total,
        bias1_total,
        gain2_total,
        bias2_total,
        qkv_final,
        outproj_final,
        up_final,
        down_final,
    )


def solution(mesh):
    placed = (
        P("dp", "band", None, None),
        P("dp", None),
        P("band", None, None),
        P(),
        P(),
        P(),
        P(),
        P(),
        P(),
        P(),
        P(),
        P(),
        P(("dp", "band"), None, None),
    )
    return jax.shard_map(
        shards,
        mesh=mesh,
        in_specs=placed,
        out_specs=(
            P(("dp", "band"), None, None),
            P("dp", "band", None, None),
            P("band", None, None),
            P(),
            P(),
            P(),
            P(),
            P(),
            P("band", "dp"),
            P("band", "dp"),
            P("band", "dp"),
            P("band", "dp"),
        ),
        check_vma=False,
    )
```

profile of v0, /device:TPU:0, one launch (start us, length us, event | category | flops | bytes accessed | tf_op | source)
XLA Modules:
  0.0 933.2 jit_solution(3808792814113410698)
XLA Ops:
  7.3 4.1 convolution_convert_fusion.4
  12.7 3.6 convolution_bitcast_fusion.1
  18.8 60.3 %reduce-scatter.18.cloned.1.call-done = f32[12,64,768]{2,1,0:T(8,128)} async-done(((f32[24,64,768]{2,1,0:T(8,128)}), f32[12,64,768]{2,1,0:T(8,128)}) %reduce-scatter.18.cloned.1.call-update) | async-done | bytes 2359312 | tf_op jit(solution)/shard_map/reduce_scatter | solution.py:50
  86.3 4.3 add_convert_fusion.1
  93.8 6.7 convolution_convert_fusion
  100.5 11.8 %reshape.239 = bf16[12,65,3,12,64]{4,3,2,1,0:T(8,128)(2,1)} reshape(bf16[780,2304]{1,0:T(8,128)(2,1)} %convolution_convert_fusion) | data formatting | bytes 7188480 | tf_op jit(solution)/shard_map/reshape | solution.py:60
  112.3 6.9 fusion.88
  119.2 5.0 copy.89
  124.2 5.0 copy.88
  129.3 5.3 copy.90
  134.6 4.0 multiply_reduce_fusion.1
  144.9 5.4 copy.59
  150.2 5.0 reshape.240
  155.2 3.7 fusion.89
  160.0 7.0 fusion.84
  167.0 26.9 %add_convert_fusion = (bf16[780,3072]{1,0:T(8,128)(2,1)S(1)}, f32[780,3072]{1,0:T(8,128)}) fusion(f32[780,3072]{1,0:T(8,128)S(1)} %fusion.84, bf16[780,768]{1,0:T(8,128)(2,1)S(1)} %copy-done.5, bf16[3072,768]{1,0:T(8,128)(2,1)S(1)} %bitcast.115), kind=kOutput, calls=%fused_computation.4 | convolution fusion | flops 3853025280 | bytes 29878272 | tf_op jit(solution)/shard_map/rd,fd->rf/dot_general | solution.py:85
  194.0 4.9 multiply_reduce_fusion.3
  204.9 4.7 reshape.243
  209.6 5.2 copy.60
  214.8 6.3 convolution_bitcast_fusion
  221.2 4.0 fusion.40
  225.1 12.8 %fusion.44 = bf16[12,65,1,12,64]{1,4,3,0,2:T(8,128)(2,1)} fusion(f32[12,12,65,65]{2,3,1,0:T(8,128)} %fusion.40, f32[12,12,65,65]{2,3,1,0:T(8,128)} %copy-done.3, f32[12,12,65]{2,1,0:T(8,128)} %log_add_fusion, bf16[12,65,1,12,64]{1,4,3,0,2:T(8,128)(2,1)} %copy.90), kind=kOutput, calls=%fused_computation.70 | convolution fusion | flops 83360224 | bytes 7300800 | tf_op jit(solution)/shard_map/chqk,ckhe->cqhe/dot_general | solution.py:116
  237.9 12.0 %fusion.49 = bf16[12,65,1,12,64]{1,4,3,0,2:T(8,128)(2,1)} fusion(f32[12,12,65,65]{2,3,1,0:T(8,128)} %fusion.40, f32[12,12,65,65]{2,3,1,0:T(8,128)} %copy-done.3, f32[12,12,65]{2,1,0:T(8,128)} %log_add_fusion, bf16[12,65,1,12,64]{1,4,3,0,2:T(8,128)(2,1)} %copy.89), kind=kOutput, calls=%fused_computation.71 | convolution fusion | flops 83360224 | bytes 7300800 | tf_op jit(solution)/shard_map/chqk,cqhe->ckhe/dot_general | solution.py:119
  249.9 6.8 maximum_convert_fusion
  256.7 13.4 %copy.65 = bf16[12,65,3,12,64]{4,3,2,1,0:T(8,128)(2,1)} copy(bf16[12,65,3,12,64]{1,4,3,0,2:T(8,128)(2,1)} %maximum_convert_fusion) | data formatting | bytes 7188480 | tf_op jit(solution)/shard_map/convert_element_type | solution.py:122
  270.1 12.7 %convert_element_type.115 = bf16[780,2304]{1,0:T(8,128)(2,1)} reshape(bf16[12,65,3,12,64]{4,3,2,1,0:T(8,128)(2,1)} %copy.65) | data formatting | bytes 7188480 | tf_op jit(solution)/shard_map/convert_element_type | solution.py:122
  282.9 6.9 multiply_reduce_fusion.4
  300.0 4.1 convolution_convert_fusion.6
  306.6 8.4 convolution_convert_fusion.1
  315.5 11.2 %multiply_convert_fusion = bf16[780,3072]{1,0:T(8,128)(2,1)} fusion(f32[780,3072]{1,0:T(8,128)} %get-tuple-element.64, f32[780,3072]{1,0:T(8,128)} %copy-done.9), kind=kLoop, calls=%fused_computation.5 | loop fusion | flops 7188480 | bytes 23961600 | tf_op jit(solution)/shard_map/convert_element_type | solution.py:80
  326.7 8.8 convolution_convert_fusion.2
  336.2 9.8 %convolution_convert_fusion.3 = bf16[768,3072]{1,0:T(8,128)(2,1)} fusion(bf16[780,3072]{1,0:T(8,128)(2,1)} %copy-done.37, f32[780,768]{1,0:T(8,128)} %copy-done.8, f32[768]{0:T(1024)S(1)} %copy-done.36, f32[768]{0:T(1024)S(1)} %copy-done.29, f32[780]{0:T(1024)S(1)} %fusion.75, f32[780]{0:T(1024)S(1)} %broadcast_multiply_fusion.1), kind=kOutput, calls=%fused_computation.32 | convolution fusion | flops 3685856256 | bytes 11919456 | tf_op jit(solution)/shard_map/rd,rf->df/dot_general | solution.py:88
  346.1 4.2 fusion.61
  350.4 9.9 %reduce-scatter.22.cloned.1.call-done = bf16[384,768]{1,0:T(8,128)(2,1)} async-done(((bf16[768,768]{1,0:T(8,128)(2,1)}), bf16[384,768]{1,0:T(8,128)(2,1)}) %reduce-scatter.22.cloned.1.call-update) | async-done | bytes 589840 | tf_op jit(solution)/shard_map/reduce_scatter | solution.py:148
  362.7 47.4 %reduce-scatter.20.cloned.1.call-done = bf16[384,2304]{1,0:T(8,128)(2,1)} async-done(((bf16[768,2304]{1,0:T(8,128)(2,1)}), bf16[384,2304]{1,0:T(8,128)(2,1)}) %reduce-scatter.20.cloned.1.call-update) | async-done | bytes 1769488 | tf_op jit(solution)/shard_map/reduce_scatter | solution.py:145
  410.1 4.2 copy.80
  414.3 58.1 %reduce-scatter.26.cloned.1.call-done = bf16[1536,768]{1,0:T(8,128)(2,1)} async-done(((bf16[3072,768]{1,0:T(8,128)(2,1)}), bf16[1536,768]{1,0:T(8,128)(2,1)}) %reduce-scatter.26.cloned.1.call-update) | async-done | bytes 2359312 | tf_op jit(solution)/shard_map/reduce_scatter | solution.py:154
  472.4 4.6 copy.86
  477.2 57.4 %reduce-scatter.24.cloned.1.call-done = bf16[384,3072]{1,0:T(8,128)(2,1)} async-done(((bf16[768,3072]{1,0:T(8,128)(2,1)}), bf16[384,3072]{1,0:T(8,128)(2,1)}) %reduce-scatter.24.cloned.1.call-update) | async-done | bytes 2359312 | tf_op jit(solution)/shard_map/reduce_scatter | solution.py:151
  534.6 4.5 copy.84
  539.2 9.4 %add_convert_fusion.2 = bf16[780,768]{1,0:T(8,128)(2,1)} fusion(f32[780,768]{1,0:T(8,128)} %copy-done.8, bf16[780,3072]{1,0:T(8,128)(2,1)} %multiply_convert_fusion, bf16[3072,768]{1,0:T(8,128)(2,1)} %param.24), kind=kOutput, calls=%fused_computation.53 | convolution fusion | flops 3681699840 | bytes 13105152 | tf_op jit(solution)/shard_map/dot_general | solution.py:81
  552.0 40.1 %all-reduce = (f32[768]{0:T(1024)}, f32[768]{0:T(1024)}, f32[768]{0:T(1024)}, f32[768]{0:T(1024)}, f32[768]{0:T(1024)}) all-reduce(f32[768]{0:T(1024)S(1)} %slice_reduce_fusion, f32[768]{0:T(1024)} %get-tuple-element.50, f32[768]{0:T(1024)} %get-tuple-element.53, ...), channel_id=1, replica_groups=mesh['dp'=16,'band'=2] {'dp','band'}, use_global_device_ids=true, to_apply=%region_14.0 | all-reduce | flops 3840 | bytes 30720 | tf_op jit(solution)/shard_map/psum | solution.py:164
  592.1 9.4 %fusion.22 = f32[24,5,256,64]{2,3,1,0:T(8,128)} fusion(bf16[24,64,768]{2,1,0:T(8,128)(2,1)} %all-gather.2.cloned.1.call-done, s32[24,64]{1,0:T(8,128)S(1)} %copy-done.27, bf16[5,64,768]{2,1,0:T(8,128)(2,1)} %param.15), kind=kOutput, calls=%fused_computation.39 | convolution fusion | flops 3628990464 | bytes 10721280 | tf_op jit(solution)/shard_map/cnd,bpd->cbnp/dot_general | solution.py:140
  601.5 30.7 %all-reduce.3.cloned.1.call-done = f32[5,64,768]{2,1,0:T(8,128)} async-done(((f32[5,64,768]{2,1,0:T(8,128)}), f32[5,64,768]{2,1,0:T(8,128)}) %all-reduce.3.cloned.1.call-update) | async-done | bytes 983056 | tf_op jit(solution)/shard_map/psum | solution.py:143
  632.2 61.7 %reduce-scatter.30.cloned.1.call-done = f32[48,384]{1,0:T(8,128)} async-done(((f32[768,384]{1,0:T(8,128)}), f32[48,384]{1,0:T(8,128)}) %reduce-scatter.30.cloned.1.call-update) | async-done | bytes 73744
  693.9 72.0 %reduce-scatter.28.cloned.1.call-done = f32[144,384]{1,0:T(8,128)} async-done(((f32[2304,384]{1,0:T(8,128)}), f32[144,384]{1,0:T(8,128)}) %reduce-scatter.28.cloned.1.call-update) | async-done | bytes 221200
  766.0 79.3 %reduce-scatter.34.cloned.1.call-done = f32[48,1536]{1,0:T(8,128)} async-done(((f32[768,1536]{1,0:T(8,128)}), f32[48,1536]{1,0:T(8,128)}) %reduce-scatter.34.cloned.1.call-update) | async-done | bytes 294928
  845.2 79.1 %reduce-scatter.32.cloned.1.call-done = f32[192,384]{1,0:T(8,128)} async-done(((f32[3072,384]{1,0:T(8,128)}), f32[192,384]{1,0:T(8,128)}) %reduce-scatter.32.cloned.1.call-update) | async-done | bytes 294928
  (136 shorter events, 49.8 us)
Async XLA Ops:
  7.2 86.6 %copy-start = (bf16[768,2304]{1,0:T(8,128)(2,1)S(1)}, bf16[768,2304]{1,0:T(8,128)(2,1)}, u32[]{:S(2)}) copy-start(bf16[768,2304]{1,0:T(8,128)(2,1)} %param.21) | copy-start | bytes 10616836
  7.2 71.9 %reduce-scatter.18.cloned.1.call-start = ((), (), s32[]{:S(2)}) async-start(), calls=%async_computation.9 | async-start | bytes 7077888 | tf_op jit(solution)/shard_map/reduce_scatter | solution.py:50
  7.2 5.4 copy-start.34
  11.3 1.3 copy-start.4
  16.3 62.9 %copy-start.30 = (f32[768]{0:T(1024)S(1)}, f32[768]{0:T(1024)}, u32[]{:S(2)}) copy-start(f32[768]{0:T(1024)} %param.16) | copy-start | bytes 9220
  16.3 329.8 %all-gather.2.cloned.1.call-start = ((), (), s32[]{:S(2)}) async-start(), calls=%async_computation.10 | async-start | bytes 3538944 | tf_op jit(solution)/shard_map/all_gather | solution.py:133
  81.9 11.8 %copy-start.21 = (f32[780]{0:T(1024)}, f32[780]{0:T(1024)S(1)}, u32[]{:S(2)}) copy-start(f32[780]{0:T(1024)S(1)} %div.51) | copy-start | bytes 9364
  85.7 4.9 copy-start.19
  90.6 3.2 copy-start.23
  90.6 3.2 copy-start.25
  90.6 3.2 copy-start.31
  138.6 2.7 copy-start.3
  138.6 2.7 copy-start.14
  138.6 3.4 copy-start.10
  140.3 1.1 copy-start.16
  155.2 4.8 copy-start.28
  155.2 4.8 copy-start.35
  158.9 40.0 %copy-start.8 = (f32[780,768]{1,0:T(8,128)}, f32[780,768]{1,0:T(8,128)S(1)}, u32[]{:S(2)}) copy-start(f32[780,768]{1,0:T(8,128)S(1)} %get-tuple-element.75) | copy-start | bytes 7188484
  158.9 8.1 slice-start
  160.0 7.0 copy-start.5
  160.0 7.0 slice-start.1
  167.0 27.0 %copy-start.9 = (f32[780,3072]{1,0:T(8,128)}, f32[780,3072]{1,0:T(8,128)S(1)}, u32[]{:S(2)}) copy-start(f32[780,3072]{1,0:T(8,128)S(1)} %fusion.84) | copy-start | bytes 28753924
  167.0 27.0 %copy-start.32 = (bf16[768,3072]{1,0:T(8,128)(2,1)S(1)}, bf16[768,3072]{1,0:T(8,128)(2,1)}, u32[]{:S(2)}) copy-start(bf16[768,3072]{1,0:T(8,128)(2,1)} %param.23) | copy-start | bytes 14155780
  194.0 4.9 copy-start.37
  194.0 4.9 copy-start.18
  199.9 1.5 copy-start.1
  199.9 2.9 copy-start.33
  201.7 1.0 copy-start.13
  214.8 6.3 copy-start.11
  214.8 6.3 copy-start.12
  270.1 12.8 %copy-start.22 = (f32[780]{0:T(1024)S(1)}, f32[780]{0:T(1024)}, u32[]{:S(2)}) copy-start(f32[780]{0:T(1024)} %copy-done.21) | copy-start | bytes 9364
  282.9 6.9 copy-start.20
  282.9 6.9 copy-start.7
  282.9 6.9 copy-start.24
  282.9 6.9 copy-start.26
  289.8 1.7 copy-start.2
  289.8 2.0 copy-start.6
  299.9 60.4 %reduce-scatter.22.cloned.1.call-start = ((), (), s32[]{:S(2)}) async-start(), calls=%async_computation.13 | async-start | bytes 1769472 | tf_op jit(solution)/shard_map/reduce_scatter | solution.py:148
  304.1 106.0 %reduce-scatter.20.cloned.1.call-start = ((), (), s32[]{:S(2)}) async-start(), calls=%async_computation.12 | async-start | bytes 5308416 | tf_op jit(solution)/shard_map/reduce_scatter | solution.py:145
  315.1 157.3 %reduce-scatter.26.cloned.1.call-start = ((), (), s32[]{:S(2)}) async-start(), calls=%async_computation.15 | async-start | bytes 7077888 | tf_op jit(solution)/shard_map/reduce_scatter | solution.py:154
  335.5 0.7 copy-start.36
  335.5 199.1 %reduce-scatter.24.cloned.1.call-start = ((), (), s32[]{:S(2)}) async-start(), calls=%async_computation.14 | async-start | bytes 7077888 | tf_op jit(solution)/shard_map/reduce_scatter | solution.py:151
  346.0 286.2 %all-reduce.3.cloned.1.call-start = ((), (), s32[]{:S(2)}) async-start(), calls=%async_computation.11 | async-start | bytes 1966080 | tf_op jit(solution)/shard_map/psum | solution.py:143
  350.3 343.6 %reduce-scatter.30.cloned.1.call-start = ((), (), s32[]{:S(2)}) async-start(), calls=%async_computation.17 | async-start | bytes 1253376
  362.7 403.3 %reduce-scatter.28.cloned.1.call-start = ((), (), s32[]{:S(2)}) async-start(), calls=%async_computation.16 | async-start | bytes 3760128
  414.3 430.9 %reduce-scatter.34.cloned.1.call-start = ((), (), s32[]{:S(2)}) async-start(), calls=%async_computation.19 | async-start | bytes 5013504
  477.0 447.3 %reduce-scatter.32.cloned.1.call-start = ((), (), s32[]{:S(2)}) async-start(), calls=%async_computation.18 | async-start | bytes 5013504
  539.1 53.0 %copy-start.27 = (s32[24,64]{1,0:T(8,128)S(1)}, s32[24,64]{1,0:T(8,128)}, u32[]{:S(2)}) copy-start(s32[24,64]{1,0:T(8,128)} %param.14) | copy-start | bytes 18436
  (3 other events, 1.9 us)
Sparse Core Ops, SparseCore 0:
  16.4 62.6 reduce-scatter.17
  300.0 36.0 all-gather.1
  338.5 21.7 reduce-scatter.21
  362.4 47.6 reduce-scatter.19
  412.4 59.9 reduce-scatter.25
  474.6 59.9 reduce-scatter.23
  539.0 93.1 all-reduce.2
  636.8 57.0 reduce-scatter.29
  698.9 67.0 reduce-scatter.27
  770.7 74.4 reduce-scatter.33
  849.7 74.5 reduce-scatter.31
where the time goes:
time: 943 us; the launch traced here: 933 us
  waiting for transfers between devices  556 us (59%)
  matrix products  162 us (17%)
  local copies, waits for them, and re-layouts  124 us (13%)
  blocking collectives  40.1 us (4%)
  other arithmetic  35.2 us (4%)
  between operations  14.6 us (2%)
    unnamed x15, waiting for transfers between devices  292 us
    reduce_scatter x1, waiting for transfers between devices, shards(): lax.psum_scatter(jnp.einsum('cbvp,bpd->cvd', picked, kernels, preferred_e...  60.3 us
    reduce_scatter x1, waiting for transfers between devices, shards(): lax.psum_scatter(grad_down.astype(jnp.bfloat16), 'band', scatter_dimensio...  58.1 us
    reduce_scatter x1, waiting for transfers between devices, shards(): lax.psum_scatter(grad_up.astype(jnp.bfloat16), 'band', scatter_dimension=...  57.4 us
    reduce_scatter x1, waiting for transfers between devices, shards(): lax.psum_scatter(grad_qkv.astype(jnp.bfloat16), 'band', scatter_dimension...  47.4 us
    unnamed x88, local copies, waits for them, and re-layouts  41.1 us
    psum x1, blocking collectives, shards(): lax.psum((grad_gain1, grad_bias1, grad_gain2, grad_bias2, grad_class), ('...  40.1 us
    psum x1, waiting for transfers between devices, shards(): kernel_grads = lax.psum(kernel_part, 'dp')  30.7 us
  transfers between devices with their start and end apart: 11, of which 10 were waited for; matrix products, arithmetic and copies ran while one was open for 10% of the time, Pallas kernels for 0%

commit v1 on v0

v1 whole, which is shorter than its diff:
```python
import functools

import jax
import jax.numpy as jnp
from jax import lax
from jax.experimental import pallas as pl
from jax.experimental.pallas import tpu as pltpu
from jax.sharding import PartitionSpec as P

HEADS = 12
HEAD = 64
BF = jnp.bfloat16
F32 = jnp.float32
TAIL = 16
BLOCK = 112
KEYS = 80
LIMIT = 56 * 1024 * 1024
SCALE = HEAD ** (-0.5)


def dot(a, b):
    return jnp.dot(a, b, preferred_element_type=F32)


def dot_nt(a, b):
    return lax.dot_general(a, b, (((1,), (1,)), ((), ())), preferred_element_type=F32)


def dot_tn(a, b):
    return lax.dot_general(a, b, (((0,), (0,)), ((), ())), preferred_element_type=F32)


def params(*semantics):
    return pltpu.CompilerParams(
        vmem_limit_bytes=LIMIT, dimension_semantics=semantics if semantics else None
    )


def cost(flops, moved):
    return pl.CostEstimate(flops=int(flops), bytes_accessed=int(moved), transcendentals=0)


def pick_kernel(base_ref, seen_ref, pixel_ref, out_ref):
    patches = pixel_ref.shape[2]
    slots = seen_ref.shape[2] // 2
    ids = lax.broadcasted_iota(jnp.int32, (patches, 2 * slots), 0)
    lane = lax.broadcasted_iota(jnp.int32, (patches, 2 * slots), 1)
    hit = ids == seen_ref[0]
    first = jnp.where(hit & (lane < slots), 1.0, 0.0).astype(BF)
    second = jnp.where(hit & (lane >= slots), 1.0, 0.0).astype(BF)
    out_ref[...] = (dot(pixel_ref[0], first) + dot(pixel_ref[1], second)).astype(BF)


def pick(pixel_rows, seen_pairs, pair_base, pairs):
    chips, depth, patches = pixel_rows.shape
    wide = seen_pairs.shape[2]
    return pl.pallas_call(
        pick_kernel,
        out_shape=jax.ShapeDtypeStruct((depth, pairs * wide), BF),
        grid_spec=pltpu.PrefetchScalarGridSpec(
            num_scalar_prefetch=1,
            grid=(pairs,),
            in_specs=[
                pl.BlockSpec((1, 1, wide), lambda i, base: (base[0] + i, 0, 0)),
                pl.BlockSpec((2, depth, patches), lambda i, base: (base[0] + i, 0, 0)),
            ],
            out_specs=pl.BlockSpec((depth, wide), lambda i, base: (0, i)),
        ),
        compiler_params=params("arbitrary"),
        cost_estimate=cost(
            2 * pairs * 2 * depth * patches * 256, pairs * 2 * depth * patches * 2
        ),
        name="pick",
    )(pair_base, seen_pairs, pixel_rows)


def row_stats(values):
    average = jnp.mean(values, axis=-1, keepdims=True)
    centred = values - average
    spread = jnp.mean(centred * centred, axis=-1, keepdims=True)
    root = lax.rsqrt(spread + 1e-06)
    return centred * root, root


def norm_back(xhat, root, grad_out, gain):
    scaled = grad_out * gain
    mean_scaled = jnp.mean(scaled, axis=-1, keepdims=True)
    mean_along = jnp.mean(scaled * xhat, axis=-1, keepdims=True)
    return root * (scaled - mean_scaled - xhat * mean_along)


def head_rows(width):
    row = lax.broadcasted_iota(jnp.int32, (TAIL, width), 0)
    lane = lax.broadcasted_iota(jnp.int32, (TAIL, width), 1)
    return (lane // HEAD) == row


def two_heads(pair):
    low = lax.broadcasted_iota(jnp.int32, pair.shape, 1) < HEAD
    zero = jnp.zeros_like(pair)
    return jnp.concatenate([jnp.where(low, pair, zero), jnp.where(low, zero, pair)], axis=0)


def own_heads(stacked):
    rows = stacked.shape[0] // 2
    low = lax.broadcasted_iota(jnp.int32, (rows, stacked.shape[1]), 1) < HEAD
    return jnp.where(low, stacked[:rows], stacked[rows:])


def softmax_keys(scores, count):
    key = lax.broadcasted_iota(jnp.int32, scores.shape, 0)
    scores = jnp.where(key < count, scores * SCALE, -1e30)
    raised = jnp.exp(scores - jnp.max(scores, axis=0, keepdims=True))
    return raised * (1.0 / jnp.sum(raised, axis=0, keepdims=True))


def forward_kernel(
    chips,
    xo_ref,
    xr_ref,
    ko_ref,
    kr_ref,
    token_ref,
    gain1_ref,
    bias1_ref,
    gain2_ref,
    bias2_ref,
    wqkv_ref,
    wout_ref,
    stream_ref,
    n1_ref,
    packed_ref,
    probs_ref,
    tprobs_ref,
    att_ref,
    mid_ref,
    n2_ref,
    tatt_ref,
):
    rows, width = n1_ref.shape
    body = rows - TAIL
    slots = body // chips
    stream_ref[0:body, :] = dot_tn(xo_ref[...], ko_ref[...]) + dot_tn(xr_ref[...], kr_ref[...])
    tail_row = lax.broadcasted_iota(jnp.int32, (TAIL, width), 0)
    stream_ref[body:rows, :] = jnp.where(tail_row < chips, token_ref[...], 0.0)

    def first_norm(i, carry):
        at = pl.ds(pl.multiple_of(i * BLOCK, BLOCK), BLOCK)
        xhat, unused = row_stats(stream_ref[at, :])
        n1_ref[at, :] = (xhat * gain1_ref[...] + bias1_ref[...]).astype(BF)
        return carry

    lax.fori_loop(0, rows // BLOCK, first_norm, 0)

    def project(j, carry):
        at = pl.ds(pl.multiple_of(j * 256, 256), 256)
        packed_ref[:, at] = dot(n1_ref[...], wqkv_ref[:, at]).astype(BF)
        return carry

    lax.fori_loop(0, 3 * width // 256, project, 0)
    tail = packed_ref[body:rows, :]
    heads = head_rows(width)
    tquery = jnp.where(heads, jnp.broadcast_to(tail[0:1, 0:width], (TAIL, width)), 0).astype(BF)
    tatt_ref[...] = jnp.zeros_like(tatt_ref)

    def chip(c, carry):
        at = pl.ds(pl.multiple_of(c * slots, slots), slots)
        for p in range(width // 128):
            here = slice(128 * p, 128 * p + 128)
            there = slice(width + 128 * p, width + 128 * p + 128)
            yonder = slice(2 * width + 128 * p, 2 * width + 128 * p + 128)
            query = two_heads(packed_ref[at, here])
            key = jnp.concatenate([packed_ref[at, there], tail[:, there]], axis=0)
            val = jnp.concatenate([packed_ref[at, yonder], tail[:, yonder]], axis=0)
            probs = softmax_keys(dot_nt(key, query), slots + 1).astype(BF)
            probs_ref[c, p] = probs
            att_ref[at, here] = own_heads(dot_tn(probs, val)).astype(BF)
        key = jnp.concatenate(
            [packed_ref[at, width : 2 * width], tail[:, width : 2 * width]], axis=0
        )
        val = jnp.concatenate([packed_ref[at, 2 * width :], tail[:, 2 * width :]], axis=0)
        tprobs = softmax_keys(dot_nt(key, tquery), slots + 1).astype(BF)
        tprobs_ref[c] = tprobs
        mixed = jnp.where(heads, dot_tn(tprobs, val), 0.0)
        tatt_ref[pl.ds(c, 1), :] = jnp.sum(mixed, axis=0, keepdims=True)
        return carry

    lax.fori_loop(0, chips, chip, 0)
    att_ref[body:rows, :] = tatt_ref[...].astype(BF)

    def out_project(j, carry):
        at = pl.ds(pl.multiple_of(j * 256, 256), 256)
        mid_ref[:, at] = stream_ref[:, at] + dot(att_ref[...], wout_ref[:, at])
        return carry

    lax.fori_loop(0, width // 256, out_project, 0)

    def second_norm(i, carry):
        at = pl.ds(pl.multiple_of(i * BLOCK, BLOCK), BLOCK)
        xhat, unused = row_stats(mid_ref[at, :])
        n2_ref[at, :] = (xhat * gain2_ref[...] + bias2_ref[...]).astype(BF)
        return carry

    lax.fori_loop(0, rows // BLOCK, second_norm, 0)


def forward(chips, xo, xr, ko, kr, token, gain1, bias1, gain2, bias2, wqkv, wout):
    width = wout.shape[0]
    body = xo.shape[1]
    rows = body + TAIL
    shape = jax.ShapeDtypeStruct
    return pl.pallas_call(
        functools.partial(forward_kernel, chips),
        out_shape=(
            shape((rows, width), F32),
            shape((rows, width), BF),
            shape((rows, 3 * width), BF),
            shape((chips, width // 128, KEYS, 128), BF),
            shape((chips, KEYS, TAIL), BF),
            shape((rows, width), BF),
            shape((rows, width), F32),
            shape((rows, width), BF),
        ),
        scratch_shapes=[pltpu.VMEM((TAIL, width), F32)],
        compiler_params=params(),
        cost_estimate=cost(2 * rows * width * width * 8, 20e6),
        name="encoder_forward",
    )(xo, xr, ko, kr, token, gain1, bias1, gain2, bias2, wqkv, wout)


def mlp_kernel(
    split,
    core_ref,
    n2_ref,
    cot_ref,
    cot_t_ref,
    up_ref,
    down_ref,
    out_in_ref,
    back_in_ref,
    down_send_ref,
    down_keep_ref,
    up_send_ref,
    up_keep_ref,
    out_ref,
    back_ref,
    act_ref,
    gpre_ref,
    grad_ref,
):
    step = pl.program_id(0)

    @pl.when(step == 0)
    def _():
        out_ref[...] = out_in_ref[...]
        back_ref[...] = back_in_ref[...]

    rows = n2_ref.shape[0]
    width = n2_ref.shape[1]
    for low, high in ((0, split), (split, rows)):
        pre = dot(n2_ref[low:high, :], up_ref[...])
        gact = dot_nt(cot_ref[low:high, :], down_ref[...])
        half = 0.5 + 0.5 * lax.erf(pre * (0.5**0.5))
        bell = jnp.exp(-0.5 * pre * pre) * 0.3989422804014327
        act_ref[low:high, :] = (pre * half).astype(BF)
        gpre_ref[low:high, :] = (gact * (half + pre * bell)).astype(BF)
    down_grad = dot(cot_t_ref[...], act_ref[...]).astype(BF)
    half_rows = width // 2
    down_send_ref[...] = down_grad[:half_rows].reshape(down_send_ref.shape)
    down_keep_ref[...] = down_grad[half_rows:].reshape(down_keep_ref.shape)
    grad_ref[...] = dot_tn(gpre_ref[...], n2_ref[...]).astype(BF)
    part = grad_ref.shape[0] // 2
    core = core_ref[0]
    sent = grad_ref[pl.ds(pl.multiple_of((1 - core) * part, part), part), :]
    kept = grad_ref[pl.ds(pl.multiple_of(core * part, part), part), :]
    for b in range(2):
        cols = slice(b * half_rows, (b + 1) * half_rows)
        up_send_ref[0, 0, b] = sent[:, cols]
        up_keep_ref[0, 0, b] = kept[:, cols]
    out_ref[...] += dot(act_ref[...], down_ref[...])
    back_ref[...] += dot_nt(gpre_ref[...], up_ref[...])


def mlp(third, core, n2, cot, cot_t, up, down, out_in, back_in):
    rows, width = n2.shape
    hidden = up.shape[1]
    chunk = hidden // 8
    part = chunk // 2
    band_cols = width // 2
    shape = jax.ShapeDtypeStruct
    whole = lambda i, core: (0, 0)
    block_at = lambda i: (i // 2) * 4 + third * 2 + i % 2
    down_shape = shape((2, 2, width // 4, 2 * chunk), BF)
    down_spec = pl.BlockSpec((2, 1, width // 4, chunk), lambda i, core: (0, i // 2, 0, i % 2))
    up_shape = shape((2, 2, 2, part, band_cols), BF)
    up_spec = pl.BlockSpec(
        (1, 1, 2, part, band_cols), lambda i, core: (i // 2, i % 2, 0, 0, 0)
    )
    return pl.pallas_call(
        functools.partial(mlp_kernel, rows // 32 * 16),
        out_shape=(
            down_shape,
            down_shape,
            up_shape,
            up_shape,
            shape((rows, width), F32),
            shape((rows, width), F32),
        ),
        grid_spec=pltpu.PrefetchScalarGridSpec(
            num_scalar_prefetch=1,
            grid=(4,),
            in_specs=[
                pl.BlockSpec((rows, width), whole),
                pl.BlockSpec((rows, width), whole),
                pl.BlockSpec((width, rows), whole),
                pl.BlockSpec((width, chunk), lambda i, core: (0, block_at(i))),
                pl.BlockSpec((chunk, width), lambda i, core: (block_at(i), 0)),
                pl.BlockSpec((rows, width), whole),
                pl.BlockSpec((rows, width), whole),
            ],
            out_specs=(
                down_spec,
                down_spec,
                up_spec,
                up_spec,
                pl.BlockSpec((rows, width), whole),
                pl.BlockSpec((rows, width), whole),
            ),
            scratch_shapes=[
                pltpu.VMEM((rows, chunk), BF),
                pltpu.VMEM((rows, chunk), BF),
                pltpu.VMEM((chunk, width), BF),
            ],
        ),
        compiler_params=params("arbitrary"),
        cost_estimate=cost(2 * rows * width * hidden * 3, 25e6),
        name="mlp_both_ways",
    )(core, n2, cot, cot_t, up, down, out_in, back_in)


def spread_blocks(full_ref, send_ref, keep_ref, core, block):
    cols = full_ref.shape[1] // 2
    for z in range(4):
        for x in range(2):
            base = (z * 2 + x) * 2
            sent = full_ref[pl.ds(pl.multiple_of((base + 1 - core) * block, 16), block), :]
            kept = full_ref[pl.ds(pl.multiple_of((base + core) * block, 16), block), :]
            for b in range(2):
                send_ref[x, b, z] = sent[:, b * cols : (b + 1) * cols]
                keep_ref[x, b, z] = kept[:, b * cols : (b + 1) * cols]


def attention_back_kernel(
    chips,
    core_ref,
    back_ref,
    mid_ref,
    cot_ref,
    gain2_ref,
    wout_ref,
    att_ref,
    packed_ref,
    probs_ref,
    tprobs_ref,
    gmid_ref,
    gpacked_ref,
    out_send_ref,
    out_keep_ref,
    vec_ref,
    branch_ref,
    gatt_ref,
    full_ref,
    tgrad_ref,
    tout_ref,
):
    rows, width = mid_ref.shape
    body = rows - TAIL
    slots = body // chips

    def norm(i, carry):
        at = pl.ds(pl.multiple_of(i * BLOCK, BLOCK), BLOCK)
        xhat, root = row_stats(mid_ref[at, :])
        grad = back_ref[at, :]
        back = norm_back(xhat, root, grad, gain2_ref[...])
        total = cot_ref[at, :].astype(F32) + back
        gmid_ref[at, :] = total
        branch_ref[at, :] = total.astype(BF)
        return (
            carry[0] + jnp.sum(grad * xhat, axis=0, keepdims=True),
            carry[1] + jnp.sum(grad, axis=0, keepdims=True),
        )

    zero = jnp.zeros((1, width), F32)
    gain_sum, bias_sum = lax.fori_loop(0, rows // BLOCK, norm, (zero, zero))
    vec_ref[0:1, :] = gain_sum
    vec_ref[1:2, :] = bias_sum

    full_ref[...] = dot_tn(branch_ref[...], att_ref[...]).astype(BF)
    spread_blocks(full_ref, out_send_ref, out_keep_ref, core_ref[0], width // 16)

    gatt = dot_nt(branch_ref[...], wout_ref[...])
    gatt_ref[...] = gatt[:body].astype(BF)
    tgrad_ref[...] = gatt[body:].astype(BF).astype(F32)
    tout_ref[...] = jnp.zeros_like(tout_ref)
    tail = packed_ref[body:rows, :]
    heads = head_rows(width)
    tquery = jnp.where(heads, jnp.broadcast_to(tail[0:1, 0:width], (TAIL, width)), 0).astype(BF)

    def chip(c, carry):
        at = pl.ds(pl.multiple_of(c * slots, slots), slots)
        key_all = jnp.concatenate(
            [packed_ref[at, width : 2 * width], tail[:, width : 2 * width]], axis=0
        )
        val_all = jnp.concatenate([packed_ref[at, 2 * width :], tail[:, 2 * width :]], axis=0)
        tgrad = jnp.where(
            heads, jnp.broadcast_to(tgrad_ref[pl.ds(c, 1), :], (TAIL, width)), 0.0
        ).astype(BF)
        tprobs = tprobs_ref[c]
        wide = tprobs.astype(F32)
        gprobs = dot_nt(val_all, tgrad)
        inner = jnp.sum(gprobs * wide, axis=0, keepdims=True)
        tscores = (wide * (gprobs - inner) * SCALE).astype(BF)
        gval_tail = dot(tprobs, tgrad)
        gkey_tail = dot(tscores, tquery)
        tq = jnp.sum(jnp.where(heads, dot_tn(tscores, key_all), 0.0), axis=0, keepdims=True)
        tkeys, tvals = [], []
        for p in range(width // 128):
            here = slice(128 * p, 128 * p + 128)
            there = slice(width + 128 * p, width + 128 * p + 128)
            yonder = slice(2 * width + 128 * p, 2 * width + 128 * p + 128)
            query = two_heads(packed_ref[at, here])
            gout = two_heads(gatt_ref[at, here])
            key = key_all[:, here]
            val = val_all[:, here]
            probs = probs_ref[c, p]
            wide = probs.astype(F32)
            gval = dot(probs, gout) + gval_tail[:, here]
            gprobs = dot_nt(val, gout)
            inner = jnp.sum(gprobs * wide, axis=0, keepdims=True)
            gscores = (wide * (gprobs - inner) * SCALE).astype(BF)
            gkey = dot(gscores, query) + gkey_tail[:, here]
            gpacked_ref[at, here] = own_heads(dot_tn(gscores, key)).astype(BF)
            gpacked_ref[at, there] = gkey[:slots].astype(BF)
            gpacked_ref[at, yonder] = gval[:slots].astype(BF)
            tkeys.append(gkey[slots : slots + 1])
            tvals.append(gval[slots : slots + 1])
        tout_ref[pl.ds(c, 1), :] = jnp.concatenate([tq] + tkeys + tvals, axis=1)
        return carry

    lax.fori_loop(0, chips, chip, 0)
    gpacked_ref[body:rows, :] = tout_ref[...].astype(BF)


def attention_back(chips, core, back, mid, cot, gain2, wout, att, packed, probs, tprobs):
    rows, width = mid.shape
    shape = jax.ShapeDtypeStruct
    block = width // 16
    vmem = pl.BlockSpec(memory_space=pltpu.VMEM)
    return pl.pallas_call(
        functools.partial(attention_back_kernel, chips),
        out_shape=(
            shape((rows, width), F32),
            shape((rows, 3 * width), BF),
            shape((2, 2, 4, block, width // 2), BF),
            shape((2, 2, 4, block, width // 2), BF),
            shape((2, width), F32),
        ),
        in_specs=[pl.BlockSpec(memory_space=pltpu.SMEM)] + [vmem] * 9,
        out_specs=(vmem,) * 5,
        scratch_shapes=[
            pltpu.VMEM((rows, width), BF),
            pltpu.VMEM((rows - TAIL, width), BF),
            pltpu.VMEM((width, width), BF),
            pltpu.VMEM((TAIL, width), F32),
            pltpu.VMEM((TAIL, 3 * width), F32),
        ],
        compiler_params=params(),
        cost_estimate=cost(2 * rows * width * width * 6, 20e6),
        name="attention_back",
    )(core, back, mid, cot, gain2, wout, att, packed, probs, tprobs)


def embed_back_kernel(
    chips,
    gpacked_ref,
    wqkv_ref,
    stream_ref,
    gmid_ref,
    gain1_ref,
    xo_ref,
    xr_ref,
    ko_ref,
    kr_ref,
    kgrad_own_ref,
    kgrad_far_ref,
    pgrad_own_ref,
    pgrad_far_ref,
    vec_ref,
    back_ref,
    embed_ref,
):
    rows, width = stream_ref.shape
    body = rows - TAIL

    back_ref[...] = dot_nt(gpacked_ref[...], wqkv_ref[...])

    def norm(i, carry):
        at = pl.ds(pl.multiple_of(i * BLOCK, BLOCK), BLOCK)
        xhat, root = row_stats(stream_ref[at, :])
        grad = back_ref[at, :]
        total = gmid_ref[at, :] + norm_back(xhat, root, grad, gain1_ref[...])
        back_ref[at, :] = total
        embed_ref[at, :] = total.astype(BF)
        return (
            carry[0] + jnp.sum(grad * xhat, axis=0, keepdims=True),
            carry[1] + jnp.sum(grad, axis=0, keepdims=True),
        )

    zero = jnp.zeros((1, width), F32)
    gain_sum, bias_sum = lax.fori_loop(0, rows // BLOCK, norm, (zero, zero))
    vec_ref[0:1, :] = gain_sum
    vec_ref[1:2, :] = bias_sum
    vec_ref[2:3, :] = jnp.sum(back_ref[body:rows, :], axis=0, keepdims=True)
    grad = embed_ref[0:body, :]
    kgrad_far_ref[...] = dot(xr_ref[...], grad).astype(BF)
    kgrad_own_ref[...] = dot(xo_ref[...], grad).astype(BF)
    pgrad_far_ref[...] = dot_nt(kr_ref[...], grad).astype(BF)
    pgrad_own_ref[...] = dot_nt(ko_ref[...], grad).astype(BF)


def embed_back(chips, gpacked, wqkv, stream, gmid, gain1, xo, xr, ko, kr):
    rows, width = stream.shape
    depth, body = xo.shape
    shape = jax.ShapeDtypeStruct
    return pl.pallas_call(
        functools.partial(embed_back_kernel, chips),
        out_shape=(
            shape((depth, width), BF),
            shape((depth, width), BF),
            shape((depth, body), BF),
            shape((depth, body), BF),
            shape((3, width), F32),
        ),
        scratch_shapes=[pltpu.VMEM((rows, width), F32), pltpu.VMEM((rows, width), BF)],
        compiler_params=params(),
        cost_estimate=cost(2 * rows * width * width * 5, 15e6),
        name="embed_back",
    )(gpacked, wqkv, stream, gmid, gain1, xo, xr, ko, kr)


def qkv_grad_kernel(core_ref, gpacked_ref, n1_ref, send_ref, keep_ref, full_ref):
    tile = 384

    def step(j, carry):
        at = pl.ds(pl.multiple_of(j * tile, tile), tile)
        full_ref[at, :] = dot_tn(gpacked_ref[:, at], n1_ref[...]).astype(BF)
        return carry

    lax.fori_loop(0, full_ref.shape[0] // tile, step, 0)
    spread_blocks(full_ref, send_ref, keep_ref, core_ref[0], full_ref.shape[0] // 16)


def qkv_grad(core, gpacked, n1):
    rows, width = n1.shape
    shape = jax.ShapeDtypeStruct
    vmem = pl.BlockSpec(memory_space=pltpu.VMEM)
    block = 3 * width // 16
    return pl.pallas_call(
        qkv_grad_kernel,
        out_shape=(shape((2, 2, 4, block, width // 2), BF),) * 2,
        in_specs=[pl.BlockSpec(memory_space=pltpu.SMEM), vmem, vmem],
        out_specs=(vmem, vmem),
        scratch_shapes=[pltpu.VMEM((3 * width, width), BF)],
        compiler_params=params(),
        cost_estimate=cost(2 * rows * width * width * 3, 8e6),
        name="qkv_grad",
    )(core, gpacked, n1)


def scatter_kernel(base_ref, seen_ref, grad_ref, *rest):
    out_ref = rest[-1]
    patches = out_ref.shape[2]
    wide = seen_ref.shape[2]
    slots = wide // 2
    ids = lax.broadcasted_iota(jnp.int32, (patches, wide), 0)
    lane = lax.broadcasted_iota(jnp.int32, (patches, wide), 1)
    hit = ids == seen_ref[0]
    first = jnp.where(hit & (lane < slots), 1.0, 0.0).astype(BF)
    second = jnp.where(hit & (lane >= slots), 1.0, 0.0).astype(BF)
    out_ref[0] = dot_nt(grad_ref[...], first)
    out_ref[1] = dot_nt(grad_ref[...], second)


def scatter(grads, seen_pairs, pair_base, patches, earlier=None):
    depth = grads.shape[0]
    wide = seen_pairs.shape[2]
    pairs = grads.shape[1] // wide
    chips = 2 * seen_pairs.shape[0]
    in_specs = [
        pl.BlockSpec((1, 1, wide), lambda i, base: (base[0] + i, 0, 0)),
        pl.BlockSpec((depth, wide), lambda i, base: (0, i)),
    ]
    operands = (pair_base, seen_pairs, grads)
    alias = {}
    if earlier is not None:
        in_specs.append(pl.BlockSpec(memory_space=pl.ANY))
        operands = operands + (earlier,)
        alias = {3: 0}
    return pl.pallas_call(
        scatter_kernel,
        out_shape=jax.ShapeDtypeStruct((chips, depth, patches), F32),
        grid_spec=pltpu.PrefetchScalarGridSpec(
            num_scalar_prefetch=1,
            grid=(pairs,),
            in_specs=in_specs,
            out_specs=pl.BlockSpec((2, depth, patches), lambda i, base: (base[0] + i, 0, 0)),
        ),
        input_output_aliases=alias,
        compiler_params=params("arbitrary"),
        cost_estimate=cost(2 * pairs * 2 * depth * patches * wide, pairs * 2 * depth * patches * 4),
        name="scatter",
    )(*operands)


class Links:
    def __init__(self, mesh):
        self.count = mesh.shape["dp"]
        self.extra = self.count // 16

    def swap(self, array, where):
        if where == "band":
            return lax.ppermute(array, "band", [(0, 1), (1, 0)])
        flip = (1 << where) * self.extra
        return lax.ppermute(array, "dp", [(d, d ^ flip) for d in range(self.count)])

    def bit(self, where):
        if where == "band":
            return lax.axis_index("band")
        return (lax.axis_index("dp") // self.extra // (1 << where)) % 2

    def halve(self, array, dim, where):
        mine = self.bit(where)
        sent = lax.dynamic_index_in_dim(array, 1 - mine, dim, keepdims=False)
        kept = lax.dynamic_index_in_dim(array, mine, dim, keepdims=False)
        return self.add(kept, self.swap(sent, where))

    def add(self, a, b):
        return (a.astype(F32) + b.astype(F32)).astype(BF)

    def reduce(self, array, names, order):
        names = list(names)
        for where in order:
            dim = names.index(where)
            array = self.halve(array, dim, where)
            names.pop(dim)
        return array.astype(F32)

    def last(self, array, rows_dim):
        if self.extra == 1:
            return array
        groups = [
            [block * self.extra + i for i in range(self.extra)] for block in range(16)
        ]
        return lax.psum_scatter(
            array, "dp", scatter_dimension=rows_dim, tiled=True, axis_index_groups=groups
        )

    def total(self, array):
        if self.extra == 1:
            return array
        groups = [
            [block * self.extra + i for i in range(self.extra)] for block in range(16)
        ]
        return lax.psum(array, "dp", axis_index_groups=groups)


def shards(
    links,
    pixels,
    visible,
    kernels,
    class_token,
    norm1_gain,
    norm1_bias,
    norm2_gain,
    norm2_bias,
    attn_qkv,
    attn_out,
    mlp_up,
    mlp_down,
    cotangent,
):
    width = attn_out.shape[0]
    chips, seq = cotangent.shape[0], cotangent.shape[1]
    group_chips, bands, patches, pix = pixels.shape
    slots = visible.shape[1]
    body = chips * slots
    rows = body + TAIL
    depth = bands * pix
    pairs = chips // 2
    band = lax.axis_index("band")
    core = links.bit(0)
    core_arg = core.reshape(1).astype(jnp.int32)

    flat_kernels = kernels.reshape(depth, width)
    kernel_halves = flat_kernels.reshape(2, depth // 2, width)
    my_half = lax.dynamic_index_in_dim(kernel_halves, core, 0, keepdims=False)
    far_half = links.swap(my_half, "band")
    far_other = links.swap(far_half, 0)
    kernels_far = jnp.where(
        core == 0,
        jnp.concatenate([far_half, far_other], axis=0),
        jnp.concatenate([far_other, far_half], axis=0),
    )

    pixel_rows = jnp.swapaxes(pixels, 2, 3).reshape(group_chips, depth, patches)
    seen_pairs = visible.reshape(group_chips // 2, 1, 2 * slots)
    own_base = (band * pairs).reshape(1).astype(jnp.int32)
    far_base = ((1 - band) * pairs).reshape(1).astype(jnp.int32)
    picked_far = pick(pixel_rows, seen_pairs, far_base, pairs)
    picked_in = links.swap(picked_far, "band")
    picked_own = pick(pixel_rows, seen_pairs, own_base, pairs)

    cot_rows = jnp.concatenate(
        [
            cotangent[:, 1:, :].reshape(body, width),
            cotangent[:, 0, :],
            jnp.zeros((TAIL - chips, width), BF),
        ],
        axis=0,
    )
    cot_t = cot_rows.T.reshape(4, 2, 2, width // 16, rows)
    cot_t = jnp.swapaxes(cot_t, 0, 1)
    cot_t = jnp.concatenate(
        [
            lax.dynamic_index_in_dim(cot_t, 1 - core, 2, keepdims=False).reshape(width // 2, rows),
            lax.dynamic_index_in_dim(cot_t, core, 2, keepdims=False).reshape(width // 2, rows),
        ],
        axis=0,
    )

    row = lambda v: v.reshape(1, width)
    stream, n1, packed, probs, tprobs, att, mid, n2 = forward(
        chips,
        picked_own,
        picked_in,
        flat_kernels,
        kernels_far,
        row(class_token),
        row(norm1_gain),
        row(norm1_bias),
        row(norm2_gain),
        row(norm2_bias),
        attn_qkv,
        attn_out,
    )

    out_rows, back = mid, jnp.zeros((rows, width), F32)
    down_parts, up_parts = [], []
    for third in range(2):
        down_send, down_keep, up_send, up_keep, out_rows, back = mlp(
            third, core_arg, n2, cot_rows, cot_t, mlp_up, mlp_down, out_rows, back
        )
        down_sum = links.add(down_keep, links.swap(down_send, 0))
        up_sum = links.add(up_keep, links.swap(up_send, 0))
        down_sum = down_sum.reshape(2, 2, 2, 2, width // 16, down_sum.shape[-1])
        down_parts.append(links.reduce(down_sum, (1, "band", 3, 2), (1, "band", 2, 3)))
        up_parts.append((third, up_sum))

    block_output = jnp.concatenate(
        [
            out_rows[body : body + chips].astype(BF)[:, None, :],
            out_rows[:body].astype(BF).reshape(chips, slots, width),
        ],
        axis=1,
    )

    up_all = jnp.stack([up_parts[0][1], up_parts[1][1]], axis=1)
    up_final = links.reduce(up_all, (3, 2, 1, "band"), ("band", 1, 2, 3))

    gmid, gpacked, out_send, out_keep, vec2 = attention_back(
        chips,
        core_arg,
        back,
        mid,
        cot_rows,
        row(norm2_gain),
        attn_out,
        att,
        packed,
        probs,
        tprobs,
    )
    names = (1, "band", 3, 2)
    out_sum = links.add(out_keep, links.swap(out_send, 0))
    out_sum = out_sum.reshape((2, 2, 2, 2) + out_sum.shape[3:])
    out_final = links.reduce(out_sum, names, (1, "band", 2, 3))

    kgrad_own, kgrad_far, pgrad_own, pgrad_far, vec1 = embed_back(
        chips,
        gpacked,
        attn_qkv,
        stream,
        gmid,
        row(norm1_gain),
        picked_own,
        picked_in,
        flat_kernels,
        kernels_far,
    )
    pgrad_in = links.swap(pgrad_far, "band")
    qkv_send, qkv_keep = qkv_grad(core_arg, gpacked, n1)
    qkv_sum = links.add(qkv_keep, links.swap(qkv_send, 0))
    qkv_sum = qkv_sum.reshape((2, 2, 2, 2) + qkv_sum.shape[3:])
    qkv_final = links.reduce(qkv_sum, names, ("band", 1, 2, 3))

    partly = scatter(pgrad_own, seen_pairs, own_base, patches)
    pixel_grads = scatter(pgrad_in, seen_pairs, far_base, patches, partly)
    pixel_grads = jnp.swapaxes(
        pixel_grads.reshape(group_chips, bands, pix, patches), 2, 3
    )

    kgrad = links.add(kgrad_own, links.swap(kgrad_far, "band"))
    for where in range(4):
        kgrad = links.halve(kgrad.reshape(2, -1, width), 0, where)
    kgrad = links.total(kgrad)
    for where in (3, 2, 1, 0):
        other = links.swap(kgrad, where)
        kgrad = jnp.where(
            links.bit(where) == 0,
            jnp.concatenate([kgrad, other], axis=0),
            jnp.concatenate([other, kgrad], axis=0),
        )
    kernel_grads = kgrad.astype(F32).reshape(bands, pix, width)

    vecs = jnp.concatenate([vec1, vec2], axis=0)
    for where in (0, "band", 1, 2, 3):
        vecs = vecs + links.swap(vecs, where)
    vecs = links.total(vecs)

    down_final = jnp.concatenate(down_parts, axis=-1)
    weight = lambda part: jnp.swapaxes(links.last(part, 0), 0, 1)
    return (
        block_output,
        pixel_grads,
        kernel_grads,
        vecs[2],
        vecs[0],
        vecs[1],
        vecs[3],
        vecs[4],
        weight(qkv_final),
        weight(out_final),
        weight(up_final),
        weight(down_final),
    )


def solution(mesh):
    placed = (
        P("dp", "band", None, None),
        P("dp", None),
        P("band", None, None),
        P(),
        P(),
        P(),
        P(),
        P(),
        P(),
        P(),
        P(),
        P(),
        P(("dp", "band"), None, None),
    )
    return jax.shard_map(
        functools.partial(shards, Links(mesh)),
        mesh=mesh,
        in_specs=placed,
        out_specs=(
            P(("dp", "band"), None, None),
            P("dp", "band", None, None),
            P("band", None, None),
            P(),
            P(),
            P(),
            P(),
            P(),
            P("band", "dp"),
            P("band", "dp"),
            P("band", "dp"),
            P("band", "dp"),
        ),
        check_vma=False,
    )
```

time: 943 us -> 365 us (0.39)
  waiting for transfers between devices: 556 us -> 102 us
  Pallas kernels: 0 us -> 166 us
  matrix products: 162 us -> 0 us
  local copies, waits for them, and re-layouts: 124 us -> 19.7 us
  starting transfers between devices: 1.03 us -> 53.5 us
  blocking collectives: 40.1 us -> 0 us
  other arithmetic: 35.2 us -> 21.2 us
  between operations: 14.6 us -> 1.28 us
    unnamed x15 -> x0, waiting for transfers between devices: 292 us -> none
    reduce_scatter x5 -> x0, waiting for transfers between devices: 233 us -> none  [the longest x1 60.3 us: shards(): lax.psum_scatter(jnp.einsum('cbvp,bpd->cvd', picked, kernels, preferred_e...]
    pallas_call x0 -> x10, Pallas kernels: none -> 166 us  [the longest x2 46.9 us: mlp(): pl.pallas_call(functools.partial(mlp_kernel, rows // 32 * 16), out_shape=...]
    dot_general x22 -> x0, matrix products: 162 us -> none  [the longest x1 26.9 us: shards(): jnp.einsum('rd,fd->rf', grad_out, mlp_down, preferred_element_type=jnp.fl...]
    ppermute x0 -> x44, waiting for transfers between devices: none -> 102 us  [the longest x34 81.1 us: swap(): return lax.ppermute(array, 'dp', [(d, d ^ flip) for d in range(self.count)])]
    ppermute x0 -> x44, starting transfers between devices: none -> 53.5 us  [the longest x34 42.5 us: swap(): return lax.ppermute(array, 'dp', [(d, d ^ flip) for d in range(self.count)])]
    psum x1 -> x0, blocking collectives: 40.1 us -> none  [shards(): lax.psum((grad_gain1, grad_bias1, grad_gain2, grad_bias2, grad_class), ('...]
    unnamed x88 -> x37, local copies, waits for them, and re-layouts: 41.1 us -> 3.4 us
  transfers between devices with their start and end apart: 11 -> 44, of which waited for: 10 -> 27; matrix products, arithmetic and copies ran while one was open for 10% -> 9% of each run, Pallas kernels for 0% -> 8%
where the time goes in v1:
time: 365 us; the launch traced here: 364 us
  Pallas kernels  166 us (45%)
  waiting for transfers between devices  102 us (28%)
  starting transfers between devices  53.5 us (15%)
  other arithmetic  21.2 us (6%)
  local copies, waits for them, and re-layouts  19.7 us (5%)
    ppermute x34, waiting for transfers between devices, swap(): return lax.ppermute(array, 'dp', [(d, d ^ flip) for d in range(self.count)])  81.1 us
    pallas_call x2, Pallas kernels, mlp(): pl.pallas_call(functools.partial(mlp_kernel, rows // 32 * 16), out_shape=...  46.9 us
    ppermute x34, starting transfers between devices, swap(): return lax.ppermute(array, 'dp', [(d, d ^ flip) for d in range(self.count)])  42.5 us
    pallas_call x1, Pallas kernels, forward(): pl.pallas_call(functools.partial(forward_kernel, chips), out_shape=(shape...  39.8 us
    pallas_call x1, Pallas kernels, attention_back(): pl.pallas_call(functools.partial(attention_back_kernel, chips), out_shape...  34 us
    ppermute x10, waiting for transfers between devices, swap(): return lax.ppermute(array, 'band', [(0, 1), (1, 0)])  20.6 us
    pallas_call x1, Pallas kernels, embed_back(): pl.pallas_call(functools.partial(embed_back_kernel, chips), out_shape=(sh...  14.7 us
    ppermute x10, starting transfers between devices, swap(): return lax.ppermute(array, 'band', [(0, 1), (1, 0)])  11 us
  transfers between devices with their start and end apart: 44, of which 27 were waited for; matrix products, arithmetic and copies ran while one was open for 9% of the time, Pallas kernels for 8%

profile of v1, /device:TPU:0, one launch (start us, length us, event | category | flops | bytes accessed | tf_op | source)
XLA Modules:
  0.0 363.8 jit_solution(6698391839632885286)
XLA Ops:
  1.6 3.0 collective-permute-start.1
  6.0 5.2 %pick.3 = bf16[320,768]{1,0:T(8,128)(2,1)} custom-call(s32[1]{0:T(128)} %bitcast.4.base_ref, s32[12,1,128]{2,1,0:T(1,128)} %reshape.160.seen_ref, bf16[24,320,256]{2,1,0:T(8,128)(2,1)} %bitcast.185), custom_call_target="tpu_custom_call" | custom-call | flops 503316480 | bytes 1966080 | tf_op jit(solution)/shard_map/pick/pallas_call | solution.py:57
  13.0 1.8 copy.39
  19.9 5.1 %pick.2.xo_ref = bf16[320,768]{1,0:T(8,128)(2,1)} custom-call(s32[1]{0:T(128)} %bitcast.1.base_ref, s32[12,1,128]{2,1,0:T(1,128)} %reshape.160.seen_ref, bf16[24,320,256]{2,1,0:T(8,128)(2,1)} %bitcast.186), custom_call_target="tpu_custom_call" | custom-call | flops 503316480 | bytes 1966080 | tf_op jit(solution)/shard_map/pick/pallas_call | solution.py:57
  28.0 2.0 maximum_select_fusion.kr_ref
  30.0 39.8 %encoder_forward.1 = (f32[784,768]{1,0:T(8,128)}, bf16[784,768]{1,0:T(8,128)(2,1)}, bf16[784,2304]{1,0:T(8,128)(2,1)}, bf16[12,6,80,128]{3,2,1,0:T(8,128)(2,1)},...) custom-call(bf16[320,768]{1,0:T(8,128)(2,1)} %pick.2.xo_ref, ...), custom_call_target="tpu_custom_call" | custom-call | flops 7398752256 | bytes 20000000 | tf_op jit(solution)/shard_map/encoder_forward/pallas_call | solution.py:212
  69.8 1.6 broadcast_in_dim.10.back_in_ref
  71.4 23.3 %mlp_both_ways.2 = (bf16[2,2,192,768]{3,2,1,0:T(8,128)(2,1)}, bf16[2,2,192,768]{3,2,1,0:T(8,128)(2,1)}, bf16[2,2,2,192,384]{4,3,2,1,0:T(8,128)(2,1)}, bf16[2,2,2...) custom-call(s32[1]{0:T(128)} %bitcast.core_ref, bf16[784,768]{1,0:T(8,128)(2,1)} %get-tuple-element.44.n2_ref, ...), custom_call_target="tpu_custom_call" | custom-call | flops 11098128384 | bytes 25000000 | tf_op jit(solution)/shard_map/mlp_both_ways/pallas_call | solution.py:299
  94.7 23.7 %mlp_both_ways.3 = (bf16[2,2,192,768]{3,2,1,0:T(8,128)(2,1)}, bf16[2,2,192,768]{3,2,1,0:T(8,128)(2,1)}, bf16[2,2,2,192,384]{4,3,2,1,0:T(8,128)(2,1)}, bf16[2,2,2...) custom-call(s32[1]{0:T(128)} %bitcast.core_ref, bf16[784,768]{1,0:T(8,128)(2,1)} %get-tuple-element.44.n2_ref, ...), custom_call_target="tpu_custom_call" | custom-call | flops 11098128384 | bytes 25000000 | tf_op jit(solution)/shard_map/mlp_both_ways/pallas_call | solution.py:299
  118.4 34.0 %attention_back.1 = (f32[784,768]{1,0:T(8,128)}, bf16[784,2304]{1,0:T(8,128)(2,1)}, bf16[2,2,4,48,384]{4,3,2,1,0:T(8,128)(2,1)}, bf16[2,2,4,48,384]{4,3,2,1,0:T(8,128)(2,1)}, f32[2,768]{1,0:T(2,128)}) custom-call(s32[1]{0:T(128)} %bitcast.core_ref, f32[784,768]{1,0:T(8,128)} %get-tuple-element.49.back_ref, f32[784,768]{1,0:T(8,128)} %get-tuple-element.45.out_in_ref.mid_ref, ...), custom_call_target="tpu_custom_call" | custom-call | flops 5549064192 | bytes 20000000 | tf_op jit(solution)/shard_map/attention_back/pallas_call | solution.py:459
  152.4 14.7 %embed_back.1 = (bf16[320,768]{1,0:T(8,128)(2,1)}, bf16[320,768]{1,0:T(8,128)(2,1)}, bf16[320,768]{1,0:T(8,128)(2,1)}, bf16[320,768]{1,0:T(8,128)(2,1)}, f32[3,768]{1,0:T(4,128)}) custom-call(bf16[784,2304]{1,0:T(8,128)(2,1)} %get-tuple-element.54.gpacked_ref, bf16[768,2304]{1,0:T(8,128)(2,1)} %wqkv_ref.3, f32[784,768]{1,0:T(8,128)} %get-tuple-element.55.stream_ref, ...), custom_call_target="tpu_custom_call" | custom-call | flops 4624220160 | bytes 15000000 | tf_op jit(solution)/shard_map/embed_back/pallas_call | solution.py:535
  169.8 2.1 collective-permute-start.14
  171.9 9.8 %qkv_grad.1 = (bf16[2,2,4,144,384]{4,3,2,1,0:T(8,128)(2,1)}, bf16[2,2,4,144,384]{4,3,2,1,0:T(8,128)(2,1)}) custom-call(s32[1]{0:T(128)} %bitcast.core_ref, bf16[784,2304]{1,0:T(8,128)(2,1)} %get-tuple-element.54.gpacked_ref, bf16[784,768]{1,0:T(8,128)(2,1)} %get-tuple-element.63.n1_ref), custom_call_target="tpu_custom_call" | custom-call | flops 2774532096 | bytes 8000000 | tf_op jit(solution)/shard_map/qkv_grad/pallas_call | solution.py:568
  182.9 2.0 collective-permute-start.4
  186.6 2.2 collective-permute-done.15
  192.7 2.6 collective-permute-start.17
  195.2 5.4 %scatter.2.rest_0_ = f32[24,320,256]{2,1,0:T(8,128)} custom-call(s32[1]{0:T(128)} %bitcast.1.base_ref, s32[12,1,128]{2,1,0:T(1,128)} %reshape.160.seen_ref, bf16[320,768]{1,0:T(8,128)(2,1)} %get-tuple-element.58.grad_ref), custom_call_target="tpu_custom_call" | custom-call | flops 251658240 | bytes 3932160 | tf_op jit(solution)/shard_map/scatter/pallas_call | solution.py:609
  202.1 5.4 %scatter.3 = f32[24,320,256]{2,1,0:T(8,128)} custom-call(s32[1]{0:T(128)} %bitcast.4.base_ref, s32[12,1,128]{2,1,0:T(1,128)} %reshape.160.seen_ref, bf16[320,768]{1,0:T(8,128)(2,1)} %copy-done.9, f32[24,320,256]{2,1,0:T(8,128)} %scatter.2.rest_0_), custom_call_target="tpu_custom_call", output_to_operand_aliasing={{}: (3, {})} | custom-call | flops 251658240 | bytes 3932160 | tf_op jit(solution)/shard_map/scatter/pallas_call | solution.py:609
  208.6 2.2 collective-permute-done.5
  212.6 4.0 %collective-permute-done.6 = bf16[80,768]{1,0:T(8,128)(2,1)S(1)} collective-permute-done((bf16[80,768]{1,0:T(8,128)(2,1)S(1)}, bf16[80,768]{1,0:T(8,128)(2,1)S(1)}, u32[]{:S(2)}, u32[]{:S(2)}) %collective-permute-start.6) | collective-permute-done | bytes 122912 | tf_op jit(solution)/shard_map/ppermute | solution.py:634
  218.1 6.9 %collective-permute-done.24 = bf16[2,2,2,48,384]{4,3,1,2,0:T(8,128)(2,1)S(1)} collective-permute-done((bf16[2,2,2,48,384]{4,3,1,2,0:T(8,128)(2,1)S(1)}, bf16[2,2,2,48,384]{4,3,1,2,0:T(8,128)(2,1)S(1)}, u32[]{:S(2)}, u32[]{:S(2)}) %collective-permute-start.24) | collective-permute-done | bytes 294944 | tf_op jit(solution)/shard_map/ppermute | solution.py:634
  225.0 1.6 collective-permute-start.7
  227.4 1.8 collective-permute-done.7
  234.1 3.0 collective-permute-done.8
  238.4 3.8 %collective-permute-done.25 = bf16[2,2,48,384]{3,2,0,1:T(8,128)(2,1)S(1)} collective-permute-done((bf16[2,2,48,384]{3,2,0,1:T(8,128)(2,1)S(1)}, bf16[2,2,48,384]{3,2,0,1:T(8,128)(2,1)S(1)}, u32[]{:S(2)}, u32[]{:S(2)}) %collective-permute-start.25) | collective-permute-done | bytes 147488 | tf_op jit(solution)/shard_map/ppermute | solution.py:632
  244.2 3.0 collective-permute-done.9
  247.1 1.7 collective-permute-start.26
  248.8 3.0 collective-permute-done.26
  253.2 2.9 collective-permute-done.10
  257.0 4.0 %collective-permute-done.27 = bf16[48,384]{1,0:T(8,128)(2,1)S(1)} collective-permute-done((bf16[48,384]{1,0:T(8,128)(2,1)S(1)}, bf16[48,384]{1,0:T(8,128)(2,1)S(1)}, u32[]{:S(2)}, u32[]{:S(2)}) %collective-permute-start.27) | collective-permute-done | bytes 36896 | tf_op jit(solution)/shard_map/ppermute | solution.py:634
  263.1 2.7 collective-permute-done.11
  267.7 1.6 add_convert_fusion.1
  275.2 10.6 %collective-permute-done.35 = bf16[2,2,2,48,768]{4,3,1,2,0:T(8,128)(2,1)S(1)} collective-permute-done((bf16[2,2,2,48,768]{4,3,1,2,0:T(8,128)(2,1)S(1)}, bf16[2,2,2,48,768]{4,3,1,2,0:T(8,128)(2,1)S(1)}, u32[]{:S(2)}, u32[]{:S(2)}) %collective-permute-start.35) | collective-permute-done | bytes 589856 | tf_op jit(solution)/shard_map/ppermute | solution.py:634
  286.7 10.9 %collective-permute-done.40 = bf16[2,2,2,48,768]{4,3,1,2,0:T(8,128)(2,1)S(1)} collective-permute-done((bf16[2,2,2,48,768]{4,3,1,2,0:T(8,128)(2,1)S(1)}, bf16[2,2,2,48,768]{4,3,1,2,0:T(8,128)(2,1)S(1)}, u32[]{:S(2)}, u32[]{:S(2)}) %collective-permute-start.40) | collective-permute-done | bytes 589856 | tf_op jit(solution)/shard_map/ppermute | solution.py:634
  300.7 8.1 %collective-permute-done.36 = bf16[2,2,48,768]{3,2,0,1:T(8,128)(2,1)S(1)} collective-permute-done((bf16[2,2,48,768]{3,2,0,1:T(8,128)(2,1)S(1)}, bf16[2,2,48,768]{3,2,0,1:T(8,128)(2,1)S(1)}, u32[]{:S(2)}, u32[]{:S(2)}) %collective-permute-start.36) | collective-permute-done | bytes 294944 | tf_op jit(solution)/shard_map/ppermute | solution.py:632
  310.2 4.8 %collective-permute-done.41 = bf16[2,2,48,768]{3,2,0,1:T(8,128)(2,1)S(1)} collective-permute-done((bf16[2,2,48,768]{3,2,0,1:T(8,128)(2,1)S(1)}, bf16[2,2,48,768]{3,2,0,1:T(8,128)(2,1)S(1)}, u32[]{:S(2)}, u32[]{:S(2)}) %collective-permute-start.41) | collective-permute-done | bytes 294944 | tf_op jit(solution)/shard_map/ppermute | solution.py:632
  316.6 1.7 collective-permute-start.38
  318.3 2.9 collective-permute-done.42
  321.4 1.9 collective-permute-done.38
  323.3 3.3 collective-permute-done.43
  328.6 3.9 %collective-permute-done.19 = bf16[2,2,2,144,384]{4,3,1,2,0:T(8,128)(2,1)S(1)} collective-permute-done((bf16[2,2,2,144,384]{4,3,1,2,0:T(8,128)(2,1)S(1)}, bf16[2,2,2,144,384]{4,3,1,2,0:T(8,128)(2,1)S(1)}, u32[]{:S(2)}, u32[]{:S(2)}) %collective-permute-start.19) | collective-permute-done | bytes 884768 | tf_op jit(solution)/shard_map/ppermute | solution.py:632
  335.1 4.9 %collective-permute-done.31 = bf16[2,2,192,384]{3,2,0,1:T(8,128)(2,1)S(1)} collective-permute-done((bf16[2,2,192,384]{3,2,0,1:T(8,128)(2,1)S(1)}, bf16[2,2,192,384]{3,2,0,1:T(8,128)(2,1)S(1)}, u32[]{:S(2)}, u32[]{:S(2)}) %collective-permute-start.31) | collective-permute-done | bytes 589856 | tf_op jit(solution)/shard_map/ppermute | solution.py:634
  340.1 1.8 collective-permute-start.32
  341.9 4.5 %collective-permute-done.20 = bf16[2,2,144,384]{3,2,0,1:T(8,128)(2,1)S(1)} collective-permute-done((bf16[2,2,144,384]{3,2,0,1:T(8,128)(2,1)S(1)}, bf16[2,2,144,384]{3,2,0,1:T(8,128)(2,1)S(1)}, u32[]{:S(2)}, u32[]{:S(2)}) %collective-permute-start.20) | collective-permute-done | bytes 442400 | tf_op jit(solution)/shard_map/ppermute | solution.py:634
  348.3 6.0 %collective-permute-start.33 = (bf16[192,384]{1,0:T(8,128)(2,1)S(1)}, bf16[192,384]{1,0:T(8,128)(2,1)S(1)}, u32[]{:S(2)}, u32[]{:S(2)}) collective-permute-start(bf16[192,384]{1,0:T(8,128)(2,1)S(1)} %dynamic-slice_bitcast_fusion.12), channel_id=1, source_target_pairs={{0,16},{2,18},{4,20},{6,22},{8,24},{10,26},{12,28},{14,30},{16,0},... | collective-permute-start | bytes 442376 | tf_op jit(solution)/shard_map/ppermute | solution.py:634
  354.4 3.4 collective-permute-start.22
  357.9 2.9 collective-permute-done.33
  361.5 1.6 collective-permute-done.22
  (184 shorter events, 63.5 us)
Async XLA Ops:
  1.6 24.6 %collective-permute-start.1 = (bf16[160,768]{1,0:T(8,128)(2,1)S(1)}, bf16[160,768]{1,0:T(8,128)(2,1)}, u32[]{:S(2)}, u32[]{:S(2)}) collective-permute-start(bf16[160,768]{1,0:T(8,128)(2,1)S(1)} %dynamic-slice_bitcast_fusion.8), channel_id=1, source_target_pairs={{0,1},{1,0},{2,3},{3,2},{4,5},{5,4},{6,7},{7,6},{8,9},{9,8},{10,11... | collective-permute-start | bytes 737288 | tf_op jit(solution)/shard_map/ppermute | solution.py:632
  11.2 18.8 %collective-permute-start = (bf16[320,768]{1,0:T(8,128)(2,1)}, bf16[320,768]{1,0:T(8,128)(2,1)}, u32[]{:S(2)}, u32[]{:S(2)}) collective-permute-start(bf16[320,768]{1,0:T(8,128)(2,1)} %pick.3), channel_id=1, source_target_pairs={{0,1},{1,0},{2,3},{3,2},{4,5},{5,4},{6,7},{7,6},{8,9},{9,8},{10,11... | collective-permute-start | bytes 1474568 | tf_op jit(solution)/shard_map/ppermute | solution.py:632
  26.2 1.7 collective-permute-start.2
  152.4 14.7 %copy-start.10 = (f32[2,768]{1,0:T(2,128)S(1)}, f32[2,768]{1,0:T(2,128)}, u32[]{:S(2)}) copy-start(f32[2,768]{1,0:T(2,128)} %get-tuple-element.62) | copy-start | bytes 18436
  167.8 1.3 collective-permute-start.13
  168.0 103.1 %collective-permute-start.28 = (bf16[2,2,2,192,384]{4,3,2,1,0:T(8,128)(2,1)}, bf16[2,2,2,192,384]{4,3,2,1,0:T(8,128)(2,1)S(1)}, u32[]{:S(2)}, u32[]{:S(2)}) collective-permute-start(bf16[2,2,2,192,384]{4,3,2,1,0:T(8,128)(2,1)} %get-tuple-element.69), channel_id=1, source_target_pairs={{0,2},{2,0},{4,6},{6,4},{8,10},{10,8},{12,14},{14,12},{16,18},{18,... | collective-permute-start | bytes 3538952 | tf_op jit(solution)/shard_map/ppermute | solution.py:634
  169.8 15.1 %collective-permute-start.14 = (f32[5,768]{1,0:T(8,128)S(1)}, f32[5,768]{1,0:T(8,128)S(1)}, u32[]{:S(2)}, u32[]{:S(2)}) collective-permute-start(f32[5,768]{1,0:T(8,128)S(1)} %fusion.30), channel_id=1, source_target_pairs={{0,1},{1,0},{2,3},{3,2},{4,5},{5,4},{6,7},{7,6},{8,9},{9,8},{10,11... | collective-permute-start | bytes 46088 | tf_op jit(solution)/shard_map/ppermute | solution.py:632
  171.9 9.8 %copy-start = (f32[784,768]{1,0:T(8,128)S(1)}, f32[784,768]{1,0:T(8,128)}, u32[]{:S(2)}) copy-start(f32[784,768]{1,0:T(8,128)} %get-tuple-element.48) | copy-start | bytes 7225348
  182.9 18.4 %collective-permute-start.3 = (bf16[320,768]{1,0:T(8,128)(2,1)S(1)}, bf16[320,768]{1,0:T(8,128)(2,1)S(1)}, u32[]{:S(2)}, u32[]{:S(2)}) collective-permute-start(bf16[320,768]{1,0:T(8,128)(2,1)S(1)} %copy-done.17), channel_id=1, source_target_pairs={{0,1},{1,0},{2,3},{3,2},{4,5},{5,4},{6,7},{7,6},{8,9},{9,8},{10,11... | collective-permute-start | bytes 1474568 | tf_op jit(solution)/shard_map/ppermute | solution.py:632
  182.9 24.5 %collective-permute-start.4 = (bf16[320,768]{1,0:T(8,128)(2,1)}, bf16[320,768]{1,0:T(8,128)(2,1)S(1)}, u32[]{:S(2)}, u32[]{:S(2)}) collective-permute-start(bf16[320,768]{1,0:T(8,128)(2,1)} %get-tuple-element.60), channel_id=1, source_target_pairs={{0,1},{1,0},{2,3},{3,2},{4,5},{5,4},{6,7},{7,6},{8,9},{9,8},{10,11... | collective-permute-start | bytes 1474568 | tf_op jit(solution)/shard_map/ppermute | solution.py:632
  184.9 3.9 %collective-permute-start.15 = (f32[5,768]{1,0:T(8,128)S(1)}, f32[5,768]{1,0:T(8,128)S(1)}, u32[]{:S(2)}, u32[]{:S(2)}) collective-permute-start(f32[5,768]{1,0:T(8,128)S(1)} %add.261), channel_id=1, source_target_pairs={{0,4},{2,6},{4,0},{6,2},{8,12},{10,14},{12,8},{14,10},{16,20},{18,... | collective-permute-start | bytes 46088 | tf_op jit(solution)/shard_map/ppermute | solution.py:634
  186.5 21.6 %collective-permute-start.23 = (bf16[2,2,4,48,384]{4,3,2,1,0:T(8,128)(2,1)S(1)}, bf16[2,2,4,48,384]{4,3,2,1,0:T(8,128)(2,1)S(1)}, u32[]{:S(2)}, u32[]{:S(2)}) collective-permute-start(bf16[2,2,4,48,384]{4,3,2,1,0:T(8,128)(2,1)S(1)} %copy-done.16), channel_id=1, source_target_pairs={{0,2},{2,0},{4,6},{6,4},{8,10},{10,8},{12,14},{14,12},{16,18},{18,... | collective-permute-start | bytes 1769480 | tf_op jit(solution)/shard_map/ppermute | solution.py:634
  188.8 3.8 %collective-permute-start.16 = (f32[5,768]{1,0:T(8,128)S(1)}, f32[5,768]{1,0:T(8,128)S(1)}, u32[]{:S(2)}, u32[]{:S(2)}) collective-permute-start(f32[5,768]{1,0:T(8,128)S(1)} %add.262), channel_id=1, source_target_pairs={{0,8},{2,10},{4,12},{6,14},{8,0},{10,2},{12,4},{14,6},{16,24},{18,... | collective-permute-start | bytes 46088 | tf_op jit(solution)/shard_map/ppermute | solution.py:634
  192.7 8.0 %collective-permute-start.17 = (f32[5,768]{1,0:T(8,128)S(1)}, f32[5,768]{1,0:T(8,128)S(1)}, u32[]{:S(2)}, u32[]{:S(2)}) collective-permute-start(f32[5,768]{1,0:T(8,128)S(1)} %add.263), channel_id=1, source_target_pairs={{0,16},{2,18},{4,20},{6,22},{8,24},{10,26},{12,28},{14,30},{16,0},... | collective-permute-start | bytes 46088 | tf_op jit(solution)/shard_map/ppermute | solution.py:634
  200.6 65.3 %collective-permute-start.34 = (bf16[2,2,192,768]{3,2,1,0:T(8,128)(2,1)}, bf16[2,2,192,768]{3,2,1,0:T(8,128)(2,1)S(1)}, u32[]{:S(2)}, u32[]{:S(2)}) collective-permute-start(bf16[2,2,192,768]{3,2,1,0:T(8,128)(2,1)} %get-tuple-element.73), channel_id=1, source_target_pairs={{0,2},{2,0},{4,6},{6,4},{8,10},{10,8},{12,14},{14,12},{16,18},{18,... | collective-permute-start | bytes 3538952 | tf_op jit(solution)/shard_map/ppermute | solution.py:634
  201.3 70.8 %collective-permute-start.29 = (bf16[2,2,2,192,384]{4,3,2,1,0:T(8,128)(2,1)}, bf16[2,2,2,192,384]{4,3,2,1,0:T(8,128)(2,1)S(1)}, u32[]{:S(2)}, u32[]{:S(2)}) collective-permute-start(bf16[2,2,2,192,384]{4,3,2,1,0:T(8,128)(2,1)} %get-tuple-element.71), channel_id=1, source_target_pairs={{0,2},{2,0},{4,6},{6,4},{8,10},{10,8},{12,14},{14,12},{16,18},{18,... | collective-permute-start | bytes 3538952 | tf_op jit(solution)/shard_map/ppermute | solution.py:634
  207.4 59.4 %collective-permute-start.39 = (bf16[2,2,192,768]{3,2,1,0:T(8,128)(2,1)}, bf16[2,2,192,768]{3,2,1,0:T(8,128)(2,1)}, u32[]{:S(2)}, u32[]{:S(2)}) collective-permute-start(bf16[2,2,192,768]{3,2,1,0:T(8,128)(2,1)} %get-tuple-element.75), channel_id=1, source_target_pairs={{0,2},{2,0},{4,6},{6,4},{8,10},{10,8},{12,14},{14,12},{16,18},{18,... | collective-permute-start | bytes 3538952 | tf_op jit(solution)/shard_map/ppermute | solution.py:634
  208.2 2.7 collective-permute-start.5
  210.9 5.7 %collective-permute-start.6 = (bf16[80,768]{1,0:T(8,128)(2,1)S(1)}, bf16[80,768]{1,0:T(8,128)(2,1)S(1)}, u32[]{:S(2)}, u32[]{:S(2)}) collective-permute-start(bf16[80,768]{1,0:T(8,128)(2,1)S(1)} %dynamic-slice_bitcast_fusion.14), channel_id=1, source_target_pairs={{0,4},{2,6},{4,0},{6,2},{8,12},{10,14},{12,8},{14,10},{16,20},{18,... | collective-permute-start | bytes 368648 | tf_op jit(solution)/shard_map/ppermute | solution.py:634
  216.6 8.5 %collective-permute-start.24 = (bf16[2,2,2,48,384]{4,3,1,2,0:T(8,128)(2,1)S(1)}, bf16[2,2,2,48,384]{4,3,1,2,0:T(8,128)(2,1)S(1)}, u32[]{:S(2)}, u32[]{:S(2)}) collective-permute-start(bf16[2,2,2,48,384]{4,3,1,2,0:T(8,128)(2,1)S(1)} %bitcast.207), channel_id=1, source_target_pairs={{0,4},{2,6},{4,0},{6,2},{8,12},{10,14},{12,8},{14,10},{16,20},{18,... | collective-permute-start | bytes 884744 | tf_op jit(solution)/shard_map/ppermute | solution.py:634
  225.0 4.2 %collective-permute-start.7 = (bf16[40,768]{1,0:T(8,128)(2,1)S(1)}, bf16[40,768]{1,0:T(8,128)(2,1)S(1)}, u32[]{:S(2)}, u32[]{:S(2)}) collective-permute-start(bf16[40,768]{1,0:T(8,128)(2,1)S(1)} %dynamic-slice_bitcast_fusion.19), channel_id=1, source_target_pairs={{0,8},{2,10},{4,12},{6,14},{8,0},{10,2},{12,4},{14,6},{16,24},{18,... | collective-permute-start | bytes 184328 | tf_op jit(solution)/shard_map/ppermute | solution.py:634
  231.4 35.1 %copy-start.4 = (bf16[2,2,192,768]{3,2,1,0:T(8,128)(2,1)S(1)}, bf16[2,2,192,768]{3,2,1,0:T(8,128)(2,1)}, u32[]{:S(2)}) copy-start(bf16[2,2,192,768]{3,2,1,0:T(8,128)(2,1)} %get-tuple-element.72) | copy-start | bytes 3538948
  232.3 4.9 %collective-permute-start.8 = (bf16[20,768]{1,0:T(8,128)(2,1)S(1)}, bf16[20,768]{1,0:T(8,128)(2,1)S(1)}, u32[]{:S(2)}, u32[]{:S(2)}) collective-permute-start(bf16[20,768]{1,0:T(8,128)(2,1)S(1)} %dynamic-slice_bitcast_fusion.21), channel_id=1, source_target_pairs={{0,16},{2,18},{4,20},{6,22},{8,24},{10,26},{12,28},{14,30},{16,0},... | collective-permute-start | bytes 92168 | tf_op jit(solution)/shard_map/ppermute | solution.py:634
  237.1 5.1 %collective-permute-start.25 = (bf16[2,2,48,384]{3,2,0,1:T(8,128)(2,1)S(1)}, bf16[2,2,48,384]{3,2,0,1:T(8,128)(2,1)S(1)}, u32[]{:S(2)}, u32[]{:S(2)}) collective-permute-start(bf16[2,2,48,384]{3,2,0,1:T(8,128)(2,1)S(1)} %dynamic-slice_bitcast_fusion.13), channel_id=1, source_target_pairs={{0,1},{1,0},{2,3},{3,2},{4,5},{5,4},{6,7},{7,6},{8,9},{9,8},{10,11... | collective-permute-start | bytes 442376 | tf_op jit(solution)/shard_map/ppermute | solution.py:632
  242.3 4.9 %collective-permute-start.9 = (bf16[20,768]{1,0:T(8,128)(2,1)S(1)}, bf16[20,768]{1,0:T(8,128)(2,1)S(1)}, u32[]{:S(2)}, u32[]{:S(2)}) collective-permute-start(bf16[20,768]{1,0:T(8,128)(2,1)S(1)} %fusion.29), channel_id=1, source_target_pairs={{0,16},{2,18},{4,20},{6,22},{8,24},{10,26},{12,28},{14,30},{16,0},... | collective-permute-start | bytes 92168 | tf_op jit(solution)/shard_map/ppermute | solution.py:634
  247.1 4.7 %collective-permute-start.26 = (bf16[2,48,384]{2,1,0:T(8,128)(2,1)S(1)}, bf16[2,48,384]{2,1,0:T(8,128)(2,1)S(1)}, u32[]{:S(2)}, u32[]{:S(2)}) collective-permute-start(bf16[2,48,384]{2,1,0:T(8,128)(2,1)S(1)} %dynamic-slice_bitcast_fusion.18), channel_id=1, source_target_pairs={{0,8},{2,10},{4,12},{6,14},{8,0},{10,2},{12,4},{14,6},{16,24},{18,... | collective-permute-start | bytes 221192 | tf_op jit(solution)/shard_map/ppermute | solution.py:634
  251.9 4.2 %collective-permute-start.10 = (bf16[40,768]{1,0:T(8,128)(2,1)S(1)}, bf16[40,768]{1,0:T(8,128)(2,1)S(1)}, u32[]{:S(2)}, u32[]{:S(2)}) collective-permute-start(bf16[40,768]{1,0:T(8,128)(2,1)S(1)} %maximum_select_fusion.4), channel_id=1, source_target_pairs={{0,8},{2,10},{4,12},{6,14},{8,0},{10,2},{12,4},{14,6},{16,24},{18,... | collective-permute-start | bytes 184328 | tf_op jit(solution)/shard_map/ppermute | solution.py:634
  256.1 4.9 %collective-permute-start.27 = (bf16[48,384]{1,0:T(8,128)(2,1)S(1)}, bf16[48,384]{1,0:T(8,128)(2,1)S(1)}, u32[]{:S(2)}, u32[]{:S(2)}) collective-permute-start(bf16[48,384]{1,0:T(8,128)(2,1)S(1)} %dynamic-slice_bitcast_fusion.20), channel_id=1, source_target_pairs={{0,16},{2,18},{4,20},{6,22},{8,24},{10,26},{12,28},{14,30},{16,0},... | collective-permute-start | bytes 110600 | tf_op jit(solution)/shard_map/ppermute | solution.py:634
  261.0 4.9 %collective-permute-start.11 = (bf16[80,768]{1,0:T(8,128)(2,1)S(1)}, bf16[80,768]{1,0:T(8,128)(2,1)S(1)}, u32[]{:S(2)}, u32[]{:S(2)}) collective-permute-start(bf16[80,768]{1,0:T(8,128)(2,1)S(1)} %maximum_select_fusion.3), channel_id=1, source_target_pairs={{0,4},{2,6},{4,0},{6,2},{8,12},{10,14},{12,8},{14,10},{16,20},{18,... | collective-permute-start | bytes 368648 | tf_op jit(solution)/shard_map/ppermute | solution.py:634
  265.8 32.5 %collective-permute-start.18 = (bf16[2,2,4,144,384]{4,3,2,1,0:T(8,128)(2,1)}, bf16[2,2,4,144,384]{4,3,2,1,0:T(8,128)(2,1)S(1)}, u32[]{:S(2)}, u32[]{:S(2)}) collective-permute-start(bf16[2,2,4,144,384]{4,3,2,1,0:T(8,128)(2,1)} %get-tuple-element.65), channel_id=1, source_target_pairs={{0,2},{2,0},{4,6},{6,4},{8,10},{10,8},{12,14},{14,12},{16,18},{18,... | collective-permute-start | bytes 5308424 | tf_op jit(solution)/shard_map/ppermute | solution.py:634
  265.9 8.2 %collective-permute-start.12 = (bf16[160,768]{1,0:T(8,128)(2,1)S(1)}, bf16[160,768]{1,0:T(8,128)(2,1)S(1)}, u32[]{:S(2)}, u32[]{:S(2)}) collective-permute-start(bf16[160,768]{1,0:T(8,128)(2,1)S(1)} %maximum_select_fusion.2), channel_id=1, source_target_pairs={{0,2},{2,0},{4,6},{6,4},{8,10},{10,8},{12,14},{14,12},{16,18},{18,... | collective-permute-start | bytes 737288 | tf_op jit(solution)/shard_map/ppermute | solution.py:634
  269.6 16.3 %collective-permute-start.35 = (bf16[2,2,2,48,768]{4,3,1,2,0:T(8,128)(2,1)S(1)}, bf16[2,2,2,48,768]{4,3,1,2,0:T(8,128)(2,1)S(1)}, u32[]{:S(2)}, u32[]{:S(2)}) collective-permute-start(bf16[2,2,2,48,768]{4,3,1,2,0:T(8,128)(2,1)S(1)} %bitcast.204), channel_id=1, source_target_pairs={{0,4},{2,6},{4,0},{6,2},{8,12},{10,14},{12,8},{14,10},{16,20},{18,... | collective-permute-start | bytes 1769480 | tf_op jit(solution)/shard_map/ppermute | solution.py:634
  271.2 26.4 %collective-permute-start.40 = (bf16[2,2,2,48,768]{4,3,1,2,0:T(8,128)(2,1)S(1)}, bf16[2,2,2,48,768]{4,3,1,2,0:T(8,128)(2,1)S(1)}, u32[]{:S(2)}, u32[]{:S(2)}) collective-permute-start(bf16[2,2,2,48,768]{4,3,1,2,0:T(8,128)(2,1)S(1)} %bitcast.203), channel_id=1, source_target_pairs={{0,4},{2,6},{4,0},{6,2},{8,12},{10,14},{12,8},{14,10},{16,20},{18,... | collective-permute-start | bytes 1769480 | tf_op jit(solution)/shard_map/ppermute | solution.py:634
  273.5 53.1 %collective-permute-start.30 = (bf16[2,2,2,192,384]{4,3,2,0,1:T(8,128)(2,1)S(1)}, bf16[2,2,2,192,384]{4,3,2,0,1:T(8,128)(2,1)S(1)}, u32[]{:S(2)}, u32[]{:S(2)}) collective-permute-start(bf16[2,2,2,192,384]{4,3,2,0,1:T(8,128)(2,1)S(1)} %fusion.5), channel_id=1, source_target_pairs={{0,1},{1,0},{2,3},{3,2},{4,5},{5,4},{6,7},{7,6},{8,9},{9,8},{10,11... | collective-permute-start | bytes 3538952 | tf_op jit(solution)/shard_map/ppermute | solution.py:632
  286.1 12.3 %copy-start.1 = (bf16[2,2,4,144,384]{4,3,2,1,0:T(8,128)(2,1)S(1)}, bf16[2,2,4,144,384]{4,3,2,1,0:T(8,128)(2,1)}, u32[]{:S(2)}) copy-start(bf16[2,2,4,144,384]{4,3,2,1,0:T(8,128)(2,1)} %get-tuple-element.64) | copy-start | bytes 5308420
  286.1 22.7 %collective-permute-start.36 = (bf16[2,2,48,768]{3,2,0,1:T(8,128)(2,1)S(1)}, bf16[2,2,48,768]{3,2,0,1:T(8,128)(2,1)S(1)}, u32[]{:S(2)}, u32[]{:S(2)}) collective-permute-start(bf16[2,2,48,768]{3,2,0,1:T(8,128)(2,1)S(1)} %dynamic-slice_bitcast_fusion.5), channel_id=1, source_target_pairs={{0,1},{1,0},{2,3},{3,2},{4,5},{5,4},{6,7},{7,6},{8,9},{9,8},{10,11... | collective-permute-start | bytes 884744 | tf_op jit(solution)/shard_map/ppermute | solution.py:632
  297.8 17.3 %collective-permute-start.41 = (bf16[2,2,48,768]{3,2,0,1:T(8,128)(2,1)S(1)}, bf16[2,2,48,768]{3,2,0,1:T(8,128)(2,1)S(1)}, u32[]{:S(2)}, u32[]{:S(2)}) collective-permute-start(bf16[2,2,48,768]{3,2,0,1:T(8,128)(2,1)S(1)} %dynamic-slice_bitcast_fusion.4), channel_id=1, source_target_pairs={{0,1},{1,0},{2,3},{3,2},{4,5},{5,4},{6,7},{7,6},{8,9},{9,8},{10,11... | collective-permute-start | bytes 884744 | tf_op jit(solution)/shard_map/ppermute | solution.py:632
  299.1 33.3 %collective-permute-start.19 = (bf16[2,2,2,144,384]{4,3,1,2,0:T(8,128)(2,1)S(1)}, bf16[2,2,2,144,384]{4,3,1,2,0:T(8,128)(2,1)S(1)}, u32[]{:S(2)}, u32[]{:S(2)}) collective-permute-start(bf16[2,2,2,144,384]{4,3,1,2,0:T(8,128)(2,1)S(1)} %bitcast.202), channel_id=1, source_target_pairs={{0,1},{1,0},{2,3},{3,2},{4,5},{5,4},{6,7},{7,6},{8,9},{9,8},{10,11... | collective-permute-start | bytes 2654216 | tf_op jit(solution)/shard_map/ppermute | solution.py:632
  308.9 7.7 %collective-permute-start.37 = (bf16[2,48,768]{2,1,0:T(8,128)(2,1)S(1)}, bf16[2,48,768]{2,1,0:T(8,128)(2,1)S(1)}, u32[]{:S(2)}, u32[]{:S(2)}) collective-permute-start(bf16[2,48,768]{2,1,0:T(8,128)(2,1)S(1)} %dynamic-slice_bitcast_fusion.11), channel_id=1, source_target_pairs={{0,8},{2,10},{4,12},{6,14},{8,0},{10,2},{12,4},{14,6},{16,24},{18,... | collective-permute-start | bytes 442376 | tf_op jit(solution)/shard_map/ppermute | solution.py:634
  315.2 6.0 %collective-permute-start.42 = (bf16[2,48,768]{2,1,0:T(8,128)(2,1)S(1)}, bf16[2,48,768]{2,1,0:T(8,128)(2,1)S(1)}, u32[]{:S(2)}, u32[]{:S(2)}) collective-permute-start(bf16[2,48,768]{2,1,0:T(8,128)(2,1)S(1)} %dynamic-slice_bitcast_fusion.10), channel_id=1, source_target_pairs={{0,8},{2,10},{4,12},{6,14},{8,0},{10,2},{12,4},{14,6},{16,24},{18,... | collective-permute-start | bytes 442376 | tf_op jit(solution)/shard_map/ppermute | solution.py:634
  316.6 6.7 %collective-permute-start.38 = (bf16[48,768]{1,0:T(8,128)(2,1)S(1)}, bf16[48,768]{1,0:T(8,128)(2,1)S(1)}, u32[]{:S(2)}, u32[]{:S(2)}) collective-permute-start(bf16[48,768]{1,0:T(8,128)(2,1)S(1)} %dynamic-slice_bitcast_fusion.17), channel_id=1, source_target_pairs={{0,16},{2,18},{4,20},{6,22},{8,24},{10,26},{12,28},{14,30},{16,0},... | collective-permute-start | bytes 221192 | tf_op jit(solution)/shard_map/ppermute | solution.py:634
  321.3 5.3 %collective-permute-start.43 = (bf16[48,768]{1,0:T(8,128)(2,1)S(1)}, bf16[48,768]{1,0:T(8,128)(2,1)S(1)}, u32[]{:S(2)}, u32[]{:S(2)}) collective-permute-start(bf16[48,768]{1,0:T(8,128)(2,1)S(1)} %dynamic-slice_bitcast_fusion.16), channel_id=1, source_target_pairs={{0,16},{2,18},{4,20},{6,22},{8,24},{10,26},{12,28},{14,30},{16,0},... | collective-permute-start | bytes 221192 | tf_op jit(solution)/shard_map/ppermute | solution.py:634
  327.0 12.9 %collective-permute-start.31 = (bf16[2,2,192,384]{3,2,0,1:T(8,128)(2,1)S(1)}, bf16[2,2,192,384]{3,2,0,1:T(8,128)(2,1)S(1)}, u32[]{:S(2)}, u32[]{:S(2)}) collective-permute-start(bf16[2,2,192,384]{3,2,0,1:T(8,128)(2,1)S(1)} %dynamic-slice_bitcast_fusion.2), channel_id=1, source_target_pairs={{0,4},{2,6},{4,0},{6,2},{8,12},{10,14},{12,8},{14,10},{16,20},{18,... | collective-permute-start | bytes 1769480 | tf_op jit(solution)/shard_map/ppermute | solution.py:634
  332.8 13.7 %collective-permute-start.20 = (bf16[2,2,144,384]{3,2,0,1:T(8,128)(2,1)S(1)}, bf16[2,2,144,384]{3,2,0,1:T(8,128)(2,1)S(1)}, u32[]{:S(2)}, u32[]{:S(2)}) collective-permute-start(bf16[2,2,144,384]{3,2,0,1:T(8,128)(2,1)S(1)} %dynamic-slice_bitcast_fusion.3), channel_id=1, source_target_pairs={{0,4},{2,6},{4,0},{6,2},{8,12},{10,14},{12,8},{14,10},{16,20},{18,... | collective-permute-start | bytes 1327112 | tf_op jit(solution)/shard_map/ppermute | solution.py:634
  340.1 8.1 %collective-permute-start.32 = (bf16[2,192,384]{2,1,0:T(8,128)(2,1)S(1)}, bf16[2,192,384]{2,1,0:T(8,128)(2,1)S(1)}, u32[]{:S(2)}, u32[]{:S(2)}) collective-permute-start(bf16[2,192,384]{2,1,0:T(8,128)(2,1)S(1)} %dynamic-slice_bitcast_fusion.6), channel_id=1, source_target_pairs={{0,8},{2,10},{4,12},{6,14},{8,0},{10,2},{12,4},{14,6},{16,24},{18,... | collective-permute-start | bytes 884744 | tf_op jit(solution)/shard_map/ppermute | solution.py:634
  346.6 7.7 %collective-permute-start.21 = (bf16[2,144,384]{2,1,0:T(8,128)(2,1)S(1)}, bf16[2,144,384]{2,1,0:T(8,128)(2,1)S(1)}, u32[]{:S(2)}, u32[]{:S(2)}) collective-permute-start(bf16[2,144,384]{2,1,0:T(8,128)(2,1)S(1)} %dynamic-slice_bitcast_fusion.9), channel_id=1, source_target_pairs={{0,8},{2,10},{4,12},{6,14},{8,0},{10,2},{12,4},{14,6},{16,24},{18,... | collective-permute-start | bytes 663560 | tf_op jit(solution)/shard_map/ppermute | solution.py:634
  348.3 12.4 %collective-permute-start.33 = (bf16[192,384]{1,0:T(8,128)(2,1)S(1)}, bf16[192,384]{1,0:T(8,128)(2,1)S(1)}, u32[]{:S(2)}, u32[]{:S(2)}) collective-permute-start(bf16[192,384]{1,0:T(8,128)(2,1)S(1)} %dynamic-slice_bitcast_fusion.12), channel_id=1, source_target_pairs={{0,16},{2,18},{4,20},{6,22},{8,24},{10,26},{12,28},{14,30},{16,0},... | collective-permute-start | bytes 442376 | tf_op jit(solution)/shard_map/ppermute | solution.py:634
  354.4 8.7 %collective-permute-start.22 = (bf16[144,384]{1,0:T(8,128)(2,1)S(1)}, bf16[144,384]{1,0:T(8,128)(2,1)S(1)}, u32[]{:S(2)}, u32[]{:S(2)}) collective-permute-start(bf16[144,384]{1,0:T(8,128)(2,1)S(1)} %dynamic-slice_bitcast_fusion.15), channel_id=1, source_target_pairs={{0,16},{2,18},{4,20},{6,22},{8,24},{10,26},{12,28},{14,30},{16,0},... | collective-permute-start | bytes 331784 | tf_op jit(solution)/shard_map/ppermute | solution.py:634
  (14 other events, 35.1 us)

commit v2 on v1

v2 whole, which is shorter than its diff:
```python
import functools

import jax
import jax.numpy as jnp
from jax import lax
from jax.experimental import pallas as pl
from jax.experimental.pallas import tpu as pltpu
from jax.sharding import PartitionSpec as P

HEADS = 12
HEAD = 64
BF = jnp.bfloat16
F32 = jnp.float32
TAIL = 16
BLOCK = 112
KEYS = 80
SCALE = HEAD ** (-0.5)


def dot(a, b):
    return jnp.dot(a, b, preferred_element_type=F32)


def dot_nt(a, b):
    return lax.dot_general(a, b, (((1,), (1,)), ((), ())), preferred_element_type=F32)


def dot_tn(a, b):
    return lax.dot_general(a, b, (((0,), (0,)), ((), ())), preferred_element_type=F32)


def params(mib, *semantics):
    return pltpu.CompilerParams(
        vmem_limit_bytes=mib * 1024 * 1024,
        dimension_semantics=semantics if semantics else None,
    )


def cost(flops, moved):
    return pl.CostEstimate(flops=int(flops), bytes_accessed=int(moved), transcendentals=0)


def chosen(seen_ref, patches):
    slots = seen_ref.shape[2] // 2
    ids = lax.broadcasted_iota(jnp.int32, (patches, 2 * slots), 0)
    lane = lax.broadcasted_iota(jnp.int32, (patches, 2 * slots), 1)
    hit = ids == seen_ref[0]
    first = jnp.where(hit & (lane < slots), 1.0, 0.0).astype(BF)
    second = jnp.where(hit & (lane >= slots), 1.0, 0.0).astype(BF)
    return first, second


def pick_kernel(where_ref, seen_ref, pixel_ref, half_ref, out_ref, half_out_ref):
    first, second = chosen(seen_ref, pixel_ref.shape[2])
    out_ref[...] = (dot(pixel_ref[0], first) + dot(pixel_ref[1], second)).astype(BF)

    @pl.when(pl.program_id(0) == 0)
    def _():
        half_out_ref[...] = half_ref[...]


def pick(where, pixel_rows, seen_pairs, halves, pairs):
    chips, depth, patches = pixel_rows.shape
    wide = seen_pairs.shape[2]
    half, width = halves.shape[1:]
    return pl.pallas_call(
        pick_kernel,
        out_shape=(
            jax.ShapeDtypeStruct((depth, pairs * wide), BF),
            jax.ShapeDtypeStruct((half, width), BF),
        ),
        grid_spec=pltpu.PrefetchScalarGridSpec(
            num_scalar_prefetch=1,
            grid=(pairs,),
            in_specs=[
                pl.BlockSpec((1, 1, wide), lambda i, w: (w[0] + i, 0, 0)),
                pl.BlockSpec((2, depth, patches), lambda i, w: (w[0] + i, 0, 0)),
                pl.BlockSpec((None, half, width), lambda i, w: (w[1], 0, 0)),
            ],
            out_specs=(
                pl.BlockSpec((depth, wide), lambda i, w: (0, i)),
                pl.BlockSpec((half, width), lambda i, w: (0, 0)),
            ),
        ),
        compiler_params=params(12, "arbitrary"),
        cost_estimate=cost(
            2 * pairs * 2 * depth * patches * 256, pairs * 2 * depth * patches * 2
        ),
        name="pick",
    )(where, seen_pairs, pixel_rows, halves)


def row_stats(values):
    average = jnp.mean(values, axis=-1, keepdims=True)
    centred = values - average
    spread = jnp.mean(centred * centred, axis=-1, keepdims=True)
    root = lax.rsqrt(spread + 1e-06)
    return centred * root, root


def norm_back(xhat, root, grad_out, gain):
    scaled = grad_out * gain
    mean_scaled = jnp.mean(scaled, axis=-1, keepdims=True)
    mean_along = jnp.mean(scaled * xhat, axis=-1, keepdims=True)
    return root * (scaled - mean_scaled - xhat * mean_along)


def head_rows(width):
    row = lax.broadcasted_iota(jnp.int32, (TAIL, width), 0)
    lane = lax.broadcasted_iota(jnp.int32, (TAIL, width), 1)
    return (lane // HEAD) == row


def two_heads(pair):
    low = lax.broadcasted_iota(jnp.int32, pair.shape, 1) < HEAD
    zero = jnp.zeros_like(pair)
    return jnp.concatenate([jnp.where(low, pair, zero), jnp.where(low, zero, pair)], axis=0)


def own_heads(stacked):
    rows = stacked.shape[0] // 2
    low = lax.broadcasted_iota(jnp.int32, (rows, stacked.shape[1]), 1) < HEAD
    return jnp.where(low, stacked[:rows], stacked[rows:])


def softmax_keys(scores, count):
    key = lax.broadcasted_iota(jnp.int32, scores.shape, 0)
    scores = jnp.where(key < count, scores * SCALE, -1e30)
    raised = jnp.exp(scores - jnp.max(scores, axis=0, keepdims=True))
    return raised * (1.0 / jnp.sum(raised, axis=0, keepdims=True))


def forward_kernel(
    chips,
    xo_ref,
    xr_ref,
    ko_ref,
    kr_ref,
    token_ref,
    gain1_ref,
    bias1_ref,
    gain2_ref,
    bias2_ref,
    wqkv_ref,
    wout_ref,
    after_ref,
    stream_ref,
    n1_ref,
    packed_ref,
    probs_ref,
    tprobs_ref,
    att_ref,
    mid_ref,
    n2_ref,
    tatt_ref,
):
    rows, width = n1_ref.shape
    body = rows - TAIL
    slots = body // chips
    stream_ref[0:body, :] = dot_tn(xo_ref[...], ko_ref[...]) + dot_tn(xr_ref[...], kr_ref[...])
    tail_row = lax.broadcasted_iota(jnp.int32, (TAIL, width), 0)
    stream_ref[body:rows, :] = jnp.where(tail_row < chips, token_ref[...], 0.0)

    def first_norm(i, carry):
        at = pl.ds(pl.multiple_of(i * BLOCK, BLOCK), BLOCK)
        xhat, unused = row_stats(stream_ref[at, :])
        n1_ref[at, :] = (xhat * gain1_ref[...] + bias1_ref[...]).astype(BF)
        return carry

    lax.fori_loop(0, rows // BLOCK, first_norm, 0)

    def project(j, carry):
        at = pl.ds(pl.multiple_of(j * 256, 256), 256)
        packed_ref[:, at] = dot(n1_ref[...], wqkv_ref[:, at]).astype(BF)
        return carry

    lax.fori_loop(0, 3 * width // 256, project, 0)
    tail = packed_ref[body:rows, :]
    heads = head_rows(width)
    tquery = jnp.where(heads, jnp.broadcast_to(tail[0:1, 0:width], (TAIL, width)), 0).astype(BF)
    tatt_ref[...] = jnp.zeros_like(tatt_ref)

    def chip(c, carry):
        at = pl.ds(pl.multiple_of(c * slots, slots), slots)
        key = jnp.concatenate(
            [packed_ref[at, width : 2 * width], tail[:, width : 2 * width]], axis=0
        )
        val = jnp.concatenate([packed_ref[at, 2 * width :], tail[:, 2 * width :]], axis=0)
        tiles = [slice(128 * p, 128 * p + 128) for p in range(width // 128)]
        scores = [dot_nt(key[:, here], two_heads(packed_ref[at, here])) for here in tiles]
        scores.append(dot_nt(key, tquery))
        probs = [softmax_keys(s, slots + 1).astype(BF) for s in scores]
        mixed = [dot_tn(probs[p], val[:, tiles[p]]) for p in range(len(tiles))]
        mixed.append(dot_tn(probs[-1], val))
        for p in range(len(tiles)):
            probs_ref[c, p] = probs[p]
            att_ref[at, tiles[p]] = own_heads(mixed[p]).astype(BF)
        tprobs_ref[c] = probs[-1]
        tatt_ref[pl.ds(c, 1), :] = jnp.sum(jnp.where(heads, mixed[-1], 0.0), axis=0, keepdims=True)
        return carry

    lax.fori_loop(0, chips, chip, 0)
    att_ref[body:rows, :] = tatt_ref[...].astype(BF)

    def out_project(j, carry):
        at = pl.ds(pl.multiple_of(j * 256, 256), 256)
        mid_ref[:, at] = stream_ref[:, at] + dot(att_ref[...], wout_ref[:, at])
        return carry

    lax.fori_loop(0, width // 256, out_project, 0)

    def second_norm(i, carry):
        at = pl.ds(pl.multiple_of(i * BLOCK, BLOCK), BLOCK)
        xhat, unused = row_stats(mid_ref[at, :])
        n2_ref[at, :] = (xhat * gain2_ref[...] + bias2_ref[...]).astype(BF)
        return carry

    lax.fori_loop(0, rows // BLOCK, second_norm, 0)


def forward(chips, xo, xr, ko, kr, token, gain1, bias1, gain2, bias2, wqkv, wout, after):
    width = wout.shape[0]
    body = xo.shape[1]
    rows = body + TAIL
    shape = jax.ShapeDtypeStruct
    return pl.pallas_call(
        functools.partial(forward_kernel, chips),
        out_shape=(
            shape((rows, width), F32),
            shape((rows, width), BF),
            shape((rows, 3 * width), BF),
            shape((chips, width // 128, KEYS, 128), BF),
            shape((chips, KEYS, TAIL), BF),
            shape((rows, width), BF),
            shape((rows, width), F32),
            shape((rows, width), BF),
        ),
        in_specs=[pl.BlockSpec(memory_space=pltpu.VMEM)] * 11
        + [pl.BlockSpec(memory_space=pl.ANY)],
        scratch_shapes=[pltpu.VMEM((TAIL, width), F32)],
        compiler_params=params(32),
        cost_estimate=cost(2 * rows * width * width * 8, 20e6),
        name="encoder_forward",
    )(xo, xr, ko, kr, token, gain1, bias1, gain2, bias2, wqkv, wout, after)


def act_grad_kernel(cot_ref, down_ref, out_ref):
    out_ref[...] = dot_nt(cot_ref[...], down_ref[...]).astype(BF)


def act_grad(cot, down):
    rows, width = cot.shape
    hidden = down.shape[0]
    chunk = hidden // 4
    return pl.pallas_call(
        act_grad_kernel,
        out_shape=jax.ShapeDtypeStruct((rows, hidden), BF),
        grid=(4,),
        in_specs=[
            pl.BlockSpec(memory_space=pltpu.VMEM),
            pl.BlockSpec((chunk, width), lambda i: (i, 0)),
        ],
        out_specs=pl.BlockSpec((rows, chunk), lambda i: (0, i)),
        compiler_params=params(12, "arbitrary"),
        cost_estimate=cost(2 * rows * width * hidden, 10e6),
        name="act_grad",
    )(cot, down)


def mlp_kernel(
    split,
    after,
    core_ref,
    n2_ref,
    cot_t_ref,
    gact_ref,
    up_ref,
    down_ref,
    out_in_ref,
    back_in_ref,
    *rest,
):
    down_send_ref, down_keep_ref, up_send_ref, up_keep_ref, out_ref, back_ref = rest[after : after + 6]
    act_ref, gpre_ref, grad_ref = rest[after + 6 :]
    step = pl.program_id(0)

    @pl.when(step == 0)
    def _():
        out_ref[...] = out_in_ref[...]
        back_ref[...] = back_in_ref[...]

    rows, width = n2_ref.shape
    half_rows = width // 2
    for low, high in ((0, split), (split, rows)):
        pre = dot(n2_ref[low:high, :], up_ref[...])
        half = 0.5 + 0.5 * lax.erf(pre * (0.5**0.5))
        bell = jnp.exp(-0.5 * pre * pre) * 0.3989422804014327
        act_ref[low:high, :] = (pre * half).astype(BF)
        gact = gact_ref[low:high, :].astype(F32)
        gpre_ref[low:high, :] = (gact * (half + pre * bell)).astype(BF)
    down_grad = dot(cot_t_ref[...], act_ref[...]).astype(BF)
    for c, ref in ((0, down_send_ref), (1, down_keep_ref)):
        for x in range(2):
            base = (c * 2 + x) * (half_rows // 2)
            for h in range(2):
                ref[x, 0, h] = down_grad[
                    base : base + half_rows // 2, h * half_rows : (h + 1) * half_rows
                ]
    grad_ref[...] = dot_tn(gpre_ref[...], n2_ref[...]).astype(BF)
    part = grad_ref.shape[0] // 4
    core = core_ref[0]
    for x in range(2):
        sent = grad_ref[pl.ds(pl.multiple_of((2 * x + 1 - core) * part, 16), part), :]
        kept = grad_ref[pl.ds(pl.multiple_of((2 * x + core) * part, 16), part), :]
        for b in range(2):
            cols = slice(b * half_rows, (b + 1) * half_rows)
            up_send_ref[0, x, b] = sent[:, cols]
            up_keep_ref[0, x, b] = kept[:, cols]
    out_ref[...] += dot(act_ref[...], down_ref[...])
    back_ref[...] += dot_nt(gpre_ref[...], up_ref[...])


def mlp(third, core, n2, cot_t, gact, up, down, out_in, back_in, after=()):
    rows, width = n2.shape
    hidden = up.shape[1]
    chunk = hidden // 4
    part = chunk // 4
    half = width // 2
    shape = jax.ShapeDtypeStruct
    vmem = pl.BlockSpec(memory_space=pltpu.VMEM)
    at = lambda i: i * 2 + third
    down_shape = shape((2, 2, 2, width // 4, half), BF)
    down_spec = pl.BlockSpec((2, 1, 2, width // 4, half), lambda i, core: (0, i, 0, 0, 0))
    up_shape = shape((2, 2, 2, part, half), BF)
    up_spec = pl.BlockSpec((1, 2, 2, part, half), lambda i, core: (i, 0, 0, 0, 0))
    return pl.pallas_call(
        functools.partial(mlp_kernel, rows // 32 * 16, len(after)),
        out_shape=(
            down_shape,
            down_shape,
            up_shape,
            up_shape,
            shape((rows, width), F32),
            shape((rows, width), F32),
        ),
        grid_spec=pltpu.PrefetchScalarGridSpec(
            num_scalar_prefetch=1,
            grid=(2,),
            in_specs=[
                vmem,
                vmem,
                pl.BlockSpec((rows, chunk), lambda i, core: (0, at(i))),
                pl.BlockSpec((width, chunk), lambda i, core: (0, at(i))),
                pl.BlockSpec((chunk, width), lambda i, core: (at(i), 0)),
                vmem,
                vmem,
            ]
            + [pl.BlockSpec(memory_space=pl.ANY)] * len(after),
            out_specs=(down_spec, down_spec, up_spec, up_spec, vmem, vmem),
            scratch_shapes=[
                pltpu.VMEM((rows, chunk), BF),
                pltpu.VMEM((rows, chunk), BF),
                pltpu.VMEM((chunk, width), BF),
            ],
        ),
        compiler_params=params(30, "arbitrary"),
        cost_estimate=cost(2 * rows * width * hidden * 3, 25e6),
        name="mlp_both_ways",
    )(core, n2, cot_t, gact, up, down, out_in, back_in, *after)


def spread_blocks(full_ref, send_refs, keep_refs, core):
    cols = full_ref.shape[1] // 2
    parts = len(send_refs)
    block = full_ref.shape[0] // 16
    piece = block // parts
    for z in range(4):
        for x in range(2):
            base = (z * 2 + x) * 2
            for refs, c in ((send_refs, 1 - core), (keep_refs, core)):
                for k in range(parts):
                    start = pl.multiple_of((base + c) * block + k * piece, 16)
                    rows = full_ref[pl.ds(start, piece), :]
                    for b in range(2):
                        refs[k][x, b, z] = rows[:, b * cols : (b + 1) * cols]


def attention_back_kernel(
    chips,
    core_ref,
    back_ref,
    mid_ref,
    cot_ref,
    gain2_ref,
    wout_ref,
    att_ref,
    packed_ref,
    probs_ref,
    tprobs_ref,
    *rest,
):
    gmid_ref, gpacked_ref, out_send_ref, out_keep_ref, vec_ref = rest[-10:-5]
    branch_ref, gatt_ref, full_ref, tgrad_ref, tout_ref = rest[-5:]
    rows, width = mid_ref.shape
    body = rows - TAIL
    slots = body // chips

    def norm(i, carry):
        at = pl.ds(pl.multiple_of(i * BLOCK, BLOCK), BLOCK)
        xhat, root = row_stats(mid_ref[at, :])
        grad = back_ref[at, :]
        back = norm_back(xhat, root, grad, gain2_ref[...])
        total = cot_ref[at, :].astype(F32) + back
        gmid_ref[at, :] = total
        branch_ref[at, :] = total.astype(BF)
        return (
            carry[0] + jnp.sum(grad * xhat, axis=0, keepdims=True),
            carry[1] + jnp.sum(grad, axis=0, keepdims=True),
        )

    zero = jnp.zeros((1, width), F32)
    gain_sum, bias_sum = lax.fori_loop(0, rows // BLOCK, norm, (zero, zero))
    vec_ref[0:1, :] = gain_sum
    vec_ref[1:2, :] = bias_sum

    full_ref[...] = dot_tn(branch_ref[...], att_ref[...]).astype(BF)
    spread_blocks(full_ref, [out_send_ref], [out_keep_ref], core_ref[0])

    gatt = dot_nt(branch_ref[...], wout_ref[...])
    gatt_ref[...] = gatt[:body].astype(BF)
    tgrad_ref[...] = gatt[body:].astype(BF).astype(F32)
    tout_ref[...] = jnp.zeros_like(tout_ref)
    tail = packed_ref[body:rows, :]
    heads = head_rows(width)
    tquery = jnp.where(heads, jnp.broadcast_to(tail[0:1, 0:width], (TAIL, width)), 0).astype(BF)

    def chip(c, carry):
        at = pl.ds(pl.multiple_of(c * slots, slots), slots)
        key_all = jnp.concatenate(
            [packed_ref[at, width : 2 * width], tail[:, width : 2 * width]], axis=0
        )
        val_all = jnp.concatenate([packed_ref[at, 2 * width :], tail[:, 2 * width :]], axis=0)
        tgrad = jnp.where(
            heads, jnp.broadcast_to(tgrad_ref[pl.ds(c, 1), :], (TAIL, width)), 0.0
        ).astype(BF)
        tprobs = tprobs_ref[c]
        tiles = [slice(128 * p, 128 * p + 128) for p in range(width // 128)]
        probs = [probs_ref[c, p] for p in range(len(tiles))] + [tprobs]
        gouts = [two_heads(gatt_ref[at, here]) for here in tiles]
        queries = [two_heads(packed_ref[at, here]) for here in tiles]
        gprobs = [dot_nt(val_all[:, tiles[p]], gouts[p]) for p in range(len(tiles))]
        gprobs.append(dot_nt(val_all, tgrad))
        gscores = []
        for prob, gprob in zip(probs, gprobs):
            wide = prob.astype(F32)
            inner = jnp.sum(gprob * wide, axis=0, keepdims=True)
            gscores.append((wide * (gprob - inner) * SCALE).astype(BF))
        gval_tail = dot(tprobs, tgrad)
        gkey_tail = dot(gscores[-1], tquery)
        mixed = jnp.where(heads, dot_tn(gscores[-1], key_all), 0.0)
        gvals = [dot(probs[p], gouts[p]) + gval_tail[:, tiles[p]] for p in range(len(tiles))]
        gkeys = [dot(gscores[p], queries[p]) + gkey_tail[:, tiles[p]] for p in range(len(tiles))]
        gqueries = [own_heads(dot_tn(gscores[p], key_all[:, tiles[p]])) for p in range(len(tiles))]
        for p in range(len(tiles)):
            gpacked_ref[at, 128 * p : 128 * p + 128] = gqueries[p].astype(BF)
            base = width + 128 * p
            gpacked_ref[at, base : base + 128] = gkeys[p][:slots].astype(BF)
            gpacked_ref[at, width + base : width + base + 128] = gvals[p][:slots].astype(BF)
        tout_ref[pl.ds(c, 1), :] = jnp.concatenate(
            [jnp.sum(mixed, axis=0, keepdims=True)]
            + [g[slots : slots + 1] for g in gkeys + gvals],
            axis=1,
        )
        return carry

    lax.fori_loop(0, chips, chip, 0)
    gpacked_ref[body:rows, :] = tout_ref[...].astype(BF)


def attention_back(chips, core, back, mid, cot, gain2, wout, att, packed, probs, tprobs, after):
    rows, width = mid.shape
    shape = jax.ShapeDtypeStruct
    block = width // 16
    vmem = pl.BlockSpec(memory_space=pltpu.VMEM)
    return pl.pallas_call(
        functools.partial(attention_back_kernel, chips),
        out_shape=(
            shape((rows, width), F32),
            shape((rows, 3 * width), BF),
            shape((2, 2, 4, block, width // 2), BF),
            shape((2, 2, 4, block, width // 2), BF),
            shape((2, width), F32),
        ),
        in_specs=[pl.BlockSpec(memory_space=pltpu.SMEM)]
        + [vmem] * 9
        + [pl.BlockSpec(memory_space=pl.ANY)] * len(after),
        out_specs=(vmem,) * 5,
        scratch_shapes=[
            pltpu.VMEM((rows, width), BF),
            pltpu.VMEM((rows - TAIL, width), BF),
            pltpu.VMEM((width, width), BF),
            pltpu.VMEM((TAIL, width), F32),
            pltpu.VMEM((TAIL, 3 * width), F32),
        ],
        compiler_params=params(32),
        cost_estimate=cost(2 * rows * width * width * 6, 20e6),
        name="attention_back",
    )(core, back, mid, cot, gain2, wout, att, packed, probs, tprobs, *after)


def embed_back_kernel(
    chips,
    bits_ref,
    gpacked_ref,
    wqkv_ref,
    stream_ref,
    gmid_ref,
    gain1_ref,
    vec2_ref,
    xo_ref,
    xr_ref,
    ko_ref,
    kr_ref,
    *rest,
):
    (
        kgrad_send_ref,
        kgrad_keep_ref,
        vec_ref,
        pgrad_own_ref,
        pgrad_far_ref,
        back_ref,
        embed_ref,
        full_ref,
    ) = rest[-8:]
    rows, width = stream_ref.shape
    body = rows - TAIL
    half = width // 2

    back_ref[...] = dot_nt(gpacked_ref[...], wqkv_ref[...])

    def norm(i, carry):
        at = pl.ds(pl.multiple_of(i * BLOCK, BLOCK), BLOCK)
        xhat, root = row_stats(stream_ref[at, :])
        grad = back_ref[at, :]
        total = gmid_ref[at, :] + norm_back(xhat, root, grad, gain1_ref[...])
        back_ref[at, :] = total
        embed_ref[at, :] = total.astype(BF)
        return (
            carry[0] + jnp.sum(grad * xhat, axis=0, keepdims=True),
            carry[1] + jnp.sum(grad, axis=0, keepdims=True),
        )

    zero = jnp.zeros((1, width), F32)
    gain_sum, bias_sum = lax.fori_loop(0, rows // BLOCK, norm, (zero, zero))
    token_sum = jnp.sum(back_ref[body:rows, :], axis=0, keepdims=True)
    vec_ref[...] = jnp.zeros_like(vec_ref)
    for i, v in enumerate((gain_sum, bias_sum, token_sum, vec2_ref[0:1, :], vec2_ref[1:2, :])):
        vec_ref[2 * i : 2 * i + 1, :] = v[:, :half]
        vec_ref[2 * i + 1 : 2 * i + 2, :] = v[:, half:]
    grad = embed_ref[0:body, :]
    depth = xo_ref.shape[0]
    core, band = bits_ref[0], bits_ref[4]
    full_ref[0] = dot(xo_ref[...], grad).astype(BF)
    full_ref[1] = dot(xr_ref[...], grad).astype(BF)
    piece = depth // 4
    for where, c, ref in ((0, 1 - core, kgrad_send_ref), (1, core, kgrad_keep_ref)):
        for far in range(2):
            for x in range(2):
                start = pl.multiple_of(c * (depth // 2) + x * piece, 16)
                block = full_ref[far, pl.ds(start, piece), :]
                for h in range(2):
                    slot = ((far + band - 2 * far * band) * 2 + x) * 2 + h
                    to = pl.ds(pl.multiple_of(slot * piece, 16), piece)
                    ref[to, :] = block[:, h * half : (h + 1) * half]
    put_vec(vec_ref[...], kgrad_send_ref, 2 * depth)
    pgrad_far_ref[...] = dot_nt(kr_ref[...], grad).astype(BF)
    pgrad_own_ref[...] = dot_nt(ko_ref[...], grad).astype(BF)


def put_vec(vec, ref, at):
    high = vec.astype(BF)
    ref[at : at + 16, :] = high
    ref[at + 16 : at + 32, :] = (vec - high.astype(F32)).astype(BF)


def get_vec(ref, at):
    return ref[at : at + 16, :].astype(F32) + ref[at + 16 : at + 32, :].astype(F32)


def embed_back(chips, bits, gpacked, wqkv, stream, gmid, gain1, vec2, xo, xr, ko, kr, after):
    rows, width = stream.shape
    depth, body = xo.shape
    shape = jax.ShapeDtypeStruct
    vmem = pl.BlockSpec(memory_space=pltpu.VMEM)
    return pl.pallas_call(
        functools.partial(embed_back_kernel, chips),
        out_shape=(
            shape((2 * depth + 32, width // 2), BF),
            shape((2 * depth, width // 2), BF),
            shape((16, width // 2), F32),
            shape((depth, body), BF),
            shape((depth, body), BF),
        ),
        in_specs=[pl.BlockSpec(memory_space=pltpu.SMEM)]
        + [vmem] * 10
        + [pl.BlockSpec(memory_space=pl.ANY)] * len(after),
        scratch_shapes=[
            pltpu.VMEM((rows, width), F32),
            pltpu.VMEM((rows, width), BF),
            pltpu.VMEM((2, depth, width), BF),
        ],
        compiler_params=params(30),
        cost_estimate=cost(2 * rows * width * width * 5, 15e6),
        name="embed_back",
    )(bits, gpacked, wqkv, stream, gmid, gain1, vec2, xo, xr, ko, kr, *after)


def qkv_grad_kernel(core_ref, gpacked_ref, n1_ref, *rest):
    sends, keeps, full_ref = rest[-7:-4], rest[-4:-1], rest[-1]
    tile = n1_ref.shape[1] // 2

    def step(j, carry):
        at = pl.ds(pl.multiple_of(j * tile, tile), tile)
        full_ref[at, :] = dot_tn(gpacked_ref[:, at], n1_ref[...]).astype(BF)
        return carry

    lax.fori_loop(0, full_ref.shape[0] // tile, step, 0)
    spread_blocks(full_ref, sends, keeps, core_ref[0])


def qkv_grad(core, gpacked, n1, after):
    rows, width = n1.shape
    shape = jax.ShapeDtypeStruct
    vmem = pl.BlockSpec(memory_space=pltpu.VMEM)
    block = width // 16
    return pl.pallas_call(
        qkv_grad_kernel,
        out_shape=(shape((2, 2, 4, block, width // 2), BF),) * 6,
        in_specs=[pl.BlockSpec(memory_space=pltpu.SMEM), vmem, vmem]
        + [pl.BlockSpec(memory_space=pl.ANY)] * len(after),
        out_specs=(vmem,) * 6,
        scratch_shapes=[pltpu.VMEM((3 * width, width), BF)],
        compiler_params=params(24),
        cost_estimate=cost(2 * rows * width * width * 3, 8e6),
        name="qkv_grad",
    )(core, gpacked, n1, *after)


def scatter_kernel(base_ref, seen_ref, grad_ref, *rest):
    out_ref = rest[-1]
    first, second = chosen(seen_ref, out_ref.shape[2])
    out_ref[0] = dot_nt(grad_ref[...], first)
    out_ref[1] = dot_nt(grad_ref[...], second)


def scatter(base, grads, seen_pairs, patches, earlier=None):
    depth = grads.shape[0]
    wide = seen_pairs.shape[2]
    pairs = grads.shape[1] // wide
    chips = 2 * seen_pairs.shape[0]
    in_specs = [
        pl.BlockSpec((1, 1, wide), lambda i, base: (base[0] + i, 0, 0)),
        pl.BlockSpec((depth, wide), lambda i, base: (0, i)),
    ]
    operands = (base, seen_pairs, grads)
    alias = {}
    if earlier is not None:
        in_specs.append(pl.BlockSpec(memory_space=pl.ANY))
        operands = operands + (earlier,)
        alias = {3: 0}
    return pl.pallas_call(
        scatter_kernel,
        out_shape=jax.ShapeDtypeStruct((chips, depth, patches), F32),
        grid_spec=pltpu.PrefetchScalarGridSpec(
            num_scalar_prefetch=1,
            grid=(pairs,),
            in_specs=in_specs,
            out_specs=pl.BlockSpec((2, depth, patches), lambda i, base: (base[0] + i, 0, 0)),
        ),
        input_output_aliases=alias,
        compiler_params=params(12, "arbitrary"),
        cost_estimate=cost(2 * pairs * 2 * depth * patches * wide, pairs * 2 * depth * patches * 4),
        name="scatter",
    )(*operands)


class Links:
    def __init__(self, mesh):
        self.count = mesh.shape["dp"]
        self.extra = self.count // 16

    def swap(self, array, where):
        if where == "band":
            return lax.ppermute(array, "band", [(0, 1), (1, 0)])
        flip = (1 << where) * self.extra
        return lax.ppermute(array, "dp", [(d, d ^ flip) for d in range(self.count)])

    def bit(self, where):
        if where == "band":
            return lax.axis_index("band")
        return (lax.axis_index("dp") // self.extra // (1 << where)) % 2

    def groups(self):
        return [[block * self.extra + i for i in range(self.extra)] for block in range(16)]

    def last(self, array):
        if self.extra == 1:
            return array
        return lax.psum_scatter(
            array, "dp", scatter_dimension=0, tiled=True, axis_index_groups=self.groups()
        )

    def total(self, array):
        if self.extra == 1:
            return array
        return lax.psum(array, "dp", axis_index_groups=self.groups())


SLOT = {0: 0, 1: 1, 2: 2, 3: 3, "band": 4}


class Piece:
    def __init__(self, names, sizes, unit, kept, recv=None, at=0, vec=False):
        self.names, self.sizes, self.unit = list(names), list(sizes), unit
        self.kept = kept if vec else kept.reshape(-1, kept.shape[-1])
        self.recv, self.at, self.vec = recv, at, vec

    def rows(self):
        count = self.unit
        for size in self.sizes:
            count = count * size
        return count

    def value(self):
        if self.vec:
            part = self.recv[self.at : self.at + 32].astype(F32)
            return self.kept + part[:16] + part[16:]
        total = self.kept.astype(F32)
        if self.recv is not None:
            total = total + self.recv[self.at : self.at + self.rows()].astype(F32)
        return total.reshape(tuple(self.sizes) + (self.unit, total.shape[-1]))


def combine_kernel(jobs, recvs, sends, bits_ref, *refs):
    kept_in = refs[: len(jobs)]
    recv_in = refs[len(jobs) : len(jobs) + recvs]
    send_out = refs[len(jobs) + recvs : len(jobs) + recvs + sends]
    kept_out = refs[len(jobs) + recvs + sends :]
    for job, kept, new in zip(jobs, kept_in, kept_out):
        recv = None if job["recv"] is None else recv_in[job["recv"]]
        send = send_out[job["send"]]
        at, to = job["at"], job["to"]
        if job["vec"]:
            total = kept[...] + get_vec(recv, at)
            new[...] = total
            put_vec(total, send, to)
            continue
        pre, post = job["pre"], job["post"]
        if pre is None:
            total = kept[...] + recv[at : at + post, :]
            new[...] = total
            send[to : to + post, :] = total
            continue
        bit = bits_ref[job["slot"]]
        for p in range(pre):
            for side, ref, start in ((1 - bit, send, to), (bit, new, 0)):
                source = (2 * p + side) * post
                total = kept[pl.ds(pl.multiple_of(source, 16), post), :]
                if recv is not None:
                    total = total + recv[pl.ds(pl.multiple_of(source + at, 16), post), :]
                ref[start + p * post : start + (p + 1) * post, :] = total


def combine(links, bits, steps):
    jobs, recv_list, kept_shapes, where_list, sizes = [], [], [], [], {}
    width = steps[0][0].kept.shape[-1]
    for piece, where, split in steps:
        if where not in where_list:
            where_list.append(where)
            sizes[where] = 0
        job = {"vec": piece.vec, "at": piece.at, "recv": None, "pre": None, "post": piece.rows()}
        if piece.recv is not None:
            found = [i for i, r in enumerate(recv_list) if r is piece.recv]
            if not found:
                recv_list.append(piece.recv)
                found = [len(recv_list) - 1]
            job["recv"] = found[0]
        job["send"], job["to"] = where_list.index(where), sizes[where]
        if piece.vec:
            sent, shape = 32, jax.ShapeDtypeStruct((16, width), F32)
        elif split:
            dim = piece.names.index(where)
            pre = 1
            for size in piece.sizes[:dim]:
                pre = pre * size
            sent = piece.rows() // 2
            job.update(pre=pre, post=sent // pre, slot=SLOT[where])
            shape = jax.ShapeDtypeStruct((sent, width), BF)
        else:
            sent = piece.rows()
            shape = jax.ShapeDtypeStruct((sent, width), BF)
        sizes[where] += sent
        kept_shapes.append(shape)
        jobs.append(job)
    vmem = pl.BlockSpec(memory_space=pltpu.VMEM)
    outs = pl.pallas_call(
        functools.partial(combine_kernel, jobs, len(recv_list), len(where_list)),
        out_shape=tuple(jax.ShapeDtypeStruct((sizes[w], width), BF) for w in where_list)
        + tuple(kept_shapes),
        in_specs=[pl.BlockSpec(memory_space=pltpu.SMEM)] + [vmem] * (len(jobs) + len(recv_list)),
        out_specs=(vmem,) * (len(where_list) + len(jobs)),
        compiler_params=params(28),
        cost_estimate=cost(1e6, 6e6),
        name="combine",
    )(bits, *[piece.kept for piece, unused, also in steps], *recv_list)
    sends = outs[: len(where_list)]
    came = [links.swap(send, where) for send, where in zip(sends, where_list)]
    for (piece, where, split), job, kept in zip(steps, jobs, outs[len(where_list) :]):
        piece.kept, piece.recv, piece.at = kept, came[job["send"]], job["to"]
        if split and not piece.vec:
            dim = piece.names.index(where)
            piece.names.pop(dim)
            piece.sizes.pop(dim)
    return sends


def shards(
    links,
    pixels,
    visible,
    kernels,
    class_token,
    norm1_gain,
    norm1_bias,
    norm2_gain,
    norm2_bias,
    attn_qkv,
    attn_out,
    mlp_up,
    mlp_down,
    cotangent,
):
    width = attn_out.shape[0]
    half = width // 2
    chips, seq = cotangent.shape[0], cotangent.shape[1]
    group_chips, bands, patches, pix = pixels.shape
    slots = visible.shape[1]
    body = chips * slots
    rows = body + TAIL
    depth = bands * pix
    pairs = chips // 2
    block = width // 16
    band = lax.axis_index("band")
    core = links.bit(0)
    core_arg = core.reshape(1).astype(jnp.int32)
    bits = jnp.stack([links.bit(w) for w in (0, 1, 2, 3, "band")]).astype(jnp.int32)

    pixel_rows = jnp.swapaxes(pixels, 2, 3).reshape(group_chips, depth, patches)
    seen_pairs = visible.reshape(group_chips // 2, 1, 2 * slots)
    own_base = (band * pairs).reshape(1).astype(jnp.int32)
    far_base = ((1 - band) * pairs).reshape(1).astype(jnp.int32)
    flat_kernels = kernels.reshape(depth, width)
    halves = flat_kernels.reshape(2, depth // 2, width)
    picked_far, my_half = pick(
        jnp.concatenate([far_base, core_arg]), pixel_rows, seen_pairs, halves, pairs
    )
    picked_in = links.swap(picked_far, "band")
    far_half = links.swap(my_half, "band")
    far_other = links.swap(far_half, 0)
    kernels_far = jnp.where(
        core == 0,
        jnp.concatenate([far_half, far_other], axis=0),
        jnp.concatenate([far_other, far_half], axis=0),
    )
    picked_own, unused_half = pick(
        jnp.concatenate([own_base, core_arg]), pixel_rows, seen_pairs, halves, pairs
    )

    cot_rows = jnp.concatenate(
        [
            cotangent[:, 1:, :].reshape(body, width),
            cotangent[:, 0, :],
            jnp.zeros((TAIL - chips, width), BF),
        ],
        axis=0,
    )
    cot_t = jnp.swapaxes(cot_rows.T.reshape(4, 2, 2, block, rows), 0, 1)
    cot_t = jnp.concatenate(
        [
            lax.dynamic_index_in_dim(cot_t, 1 - core, 2, keepdims=False).reshape(half, rows),
            lax.dynamic_index_in_dim(cot_t, core, 2, keepdims=False).reshape(half, rows),
        ],
        axis=0,
    )
    gact = act_grad(cot_rows, mlp_down)

    row = lambda v: v.reshape(1, width)
    stream, n1, packed, probs, tprobs, att, mid, n2 = forward(
        chips,
        picked_own,
        picked_in,
        flat_kernels,
        kernels_far,
        row(class_token),
        row(norm1_gain),
        row(norm1_bias),
        row(norm2_gain),
        row(norm2_bias),
        attn_qkv,
        attn_out,
        gact,
    )

    def mlp_pieces(third, out_in, back_in, after=()):
        down_send, down_keep, up_send, up_keep, out_rows, back = mlp(
            third, core_arg, n2, cot_t, gact, mlp_up, mlp_down, out_in, back_in, after
        )
        flat = lambda a: a.reshape(-1, half)
        down = Piece(
            (1, "band", "h", 3, 2), (2, 2, 2, 2, 2), block, down_keep, links.swap(flat(down_send), 0)
        )
        up = Piece((3, 1, "band"), (2, 2, 2), 4 * block, up_keep, links.swap(flat(up_send), 0))
        return down, up, out_rows, back

    down1, up1, out_rows, back = mlp_pieces(0, mid, jnp.zeros((rows, width), F32))
    down2, up2, out_rows, back = mlp_pieces(1, out_rows, back)
    tie = combine(links, bits, [(down1, 1, True), (up1, "band", True)])

    block_output = jnp.concatenate(
        [
            out_rows[body : body + chips].astype(BF)[:, None, :],
            out_rows[:body].astype(BF).reshape(chips, slots, width),
        ],
        axis=1,
    )

    gmid, gpacked, out_send, out_keep, vec2 = attention_back(
        chips,
        core_arg,
        back,
        mid,
        cot_rows,
        row(norm2_gain),
        attn_out,
        att,
        packed,
        probs,
        tprobs,
        tie,
    )
    names, sizes = (1, "band", 3, 2), (2, 2, 2, 2)
    outp = Piece(names, sizes, block, out_keep, links.swap(out_send.reshape(-1, half), 0))
    tie = combine(
        links,
        bits,
        [(down1, "band", True), (up1, 1, True), (down2, 1, True), (up2, "band", True)],
    )

    sent = qkv_grad(core_arg, gpacked, n1, tie)
    qkv = [
        Piece(names, sizes, block, keep, links.swap(send.reshape(-1, half), 0))
        for send, keep in zip(sent[:3], sent[3:])
    ]
    kg_send, kg_keep, vec_keep, pgrad_own, pgrad_far = embed_back(
        chips,
        bits,
        gpacked,
        attn_qkv,
        stream,
        gmid,
        row(norm1_gain),
        vec2,
        picked_own,
        picked_in,
        flat_kernels,
        kernels_far,
        (),
    )
    kg_in = links.swap(kg_send, 0)
    kg = Piece(("band", 1, "h"), (2, 2, 2), depth // 4, kg_keep, kg_in)
    vec = Piece((), (), 16, vec_keep, kg_in, 2 * depth, True)
    pgrad_in = links.swap(pgrad_far, "band")

    combine(
        links,
        bits,
        [
            (down1, 2, True),
            (down2, "band", True),
            (up2, 1, True),
            (outp, 1, True),
            (qkv[0], 1, True),
            (qkv[1], "band", True),
            (qkv[2], 2, True),
        ],
    )
    partly = scatter(own_base, pgrad_own, seen_pairs, patches)

    stacked = jnp.stack(
        [piece.value().astype(BF).reshape(2, 4 * block, half) for piece in (up1, up2)], axis=1
    )
    up = Piece((3, 2), (2, 2), 4 * block, stacked)
    combine(
        links,
        bits,
        [
            (kg, "band", True),
            (vec, "band", False),
            (down1, 3, True),
            (down2, 2, True),
            (up, 2, True),
            (outp, "band", True),
            (qkv[0], "band", True),
            (qkv[1], 1, True),
            (qkv[2], 3, True),
        ],
    )
    pixel_grads = scatter(far_base, pgrad_in, seen_pairs, patches, partly)
    pixel_grads = jnp.swapaxes(pixel_grads.reshape(group_chips, bands, pix, patches), 2, 3)

    combine(
        links,
        bits,
        [
            (kg, 1, True),
            (vec, 1, False),
            (down2, 3, True),
            (up, 3, True),
            (outp, 2, True),
            (qkv[0], 2, True),
            (qkv[1], 2, True),
            (qkv[2], 1, True),
        ],
    )
    combine(
        links,
        bits,
        [
            (kg, 2, False),
            (vec, 2, False),
            (outp, 3, True),
            (qkv[0], 3, True),
            (qkv[1], 3, True),
            (qkv[2], "band", True),
        ],
    )
    combine(links, bits, [(kg, 3, False), (vec, 3, False)])
    vecs = links.total(vec.value()).reshape(8, width)
    kgrad = links.total(kg.value()).astype(BF)
    for where in (1, 0):
        other = links.swap(kgrad, where)
        kgrad = jnp.where(
            links.bit(where) == 0, jnp.stack([kgrad, other]), jnp.stack([other, kgrad])
        )
    kernel_grads = jnp.transpose(kgrad.astype(F32), (0, 1, 3, 2, 4)).reshape(bands, pix, width)

    weight = lambda part: jnp.swapaxes(links.last(part), 0, 1)
    down_final = jnp.concatenate([down1.value(), down2.value()], axis=0)
    return (
        block_output,
        pixel_grads,
        kernel_grads,
        vecs[2],
        vecs[0],
        vecs[1],
        vecs[3],
        vecs[4],
        weight(jnp.concatenate([piece.value() for piece in qkv], axis=0)),
        weight(outp.value()),
        weight(up.value()),
        weight(jnp.swapaxes(down_final, 0, 1).reshape(block, 4 * half)),
    )


def solution(mesh):
    placed = (
        P("dp", "band", None, None),
        P("dp", None),
        P("band", None, None),
        P(),
        P(),
        P(),
        P(),
        P(),
        P(),
        P(),
        P(),
        P(),
        P(("dp", "band"), None, None),
    )
    return jax.shard_map(
        functools.partial(shards, Links(mesh)),
        mesh=mesh,
        in_specs=placed,
        out_specs=(
            P(("dp", "band"), None, None),
            P("dp", "band", None, None),
            P("band", None, None),
            P(),
            P(),
            P(),
            P(),
            P(),
            P("band", "dp"),
            P("band", "dp"),
            P("band", "dp"),
            P("band", "dp"),
        ),
        check_vma=False,
    )
```

time: 365 us -> 263 us (0.72)
  Pallas kernels: 166 us -> 106 us
  waiting for transfers between devices: 102 us -> 62.1 us
  local copies, waits for them, and re-layouts: 19.7 us -> 52.6 us
  starting transfers between devices: 53.5 us -> 32.1 us
  other arithmetic: 21.2 us -> 7.33 us
    unnamed x37 -> x155, local copies, waits for them, and re-layouts: 3.4 us -> 40.7 us
    ppermute x34 -> x25, waiting for transfers between devices: 81.1 us -> 47.7 us  [swap(): return lax.ppermute(array, 'dp', [(d, d ^ flip) for d in range(self.count)])]
    pallas_call x1, Pallas kernels: 39.8 us -> 17.2 us  [forward(): pl.pallas_call(functools.partial(forward_kernel, chips), out_shape=(shape...]
    pallas_call x1, Pallas kernels: 34 us -> 13.7 us  [attention_back(): pl.pallas_call(functools.partial(attention_back_kernel, chips), out_shape...]
    ppermute x34 -> x25, starting transfers between devices: 42.5 us -> 24 us  [swap(): return lax.ppermute(array, 'dp', [(d, d ^ flip) for d in range(self.count)])]
    convert_element_type x27 -> x4, other arithmetic: 8.51 us -> 0.19 us  [the longest x2 0.15 us: shards(): piece.value().astype(BF).reshape(2, 4 * block, half)]
    ppermute x10 -> x8, waiting for transfers between devices: 20.6 us -> 14.3 us  [swap(): return lax.ppermute(array, 'band', [(0, 1), (1, 0)])]
    pallas_call x1, Pallas kernels: 14.7 us -> 9.97 us  [embed_back(): pl.pallas_call(functools.partial(embed_back_kernel, chips), out_shape=(sh...]
  transfers between devices with their start and end apart: 44 -> 33, of which waited for: 27 -> 14; matrix products, arithmetic and copies ran while one was open for 9% -> 6% of each run, Pallas kernels for 8% -> 25%
where the time goes in v2:
time: 263 us; the launch traced here: 262 us
  Pallas kernels  106 us (40%)
  waiting for transfers between devices  62.1 us (24%)
  local copies, waits for them, and re-layouts  52.6 us (20%)
  starting transfers between devices  32.1 us (12%)
  other arithmetic  7.33 us (3%)
    ppermute x25, waiting for transfers between devices, swap(): return lax.ppermute(array, 'dp', [(d, d ^ flip) for d in range(self.count)])  47.7 us
    unnamed x155, local copies, waits for them, and re-layouts  40.7 us
    pallas_call x2, Pallas kernels, mlp(): pl.pallas_call(functools.partial(mlp_kernel, rows // 32 * 16, len(after))...  31 us
    ppermute x25, starting transfers between devices, swap(): return lax.ppermute(array, 'dp', [(d, d ^ flip) for d in range(self.count)])  24 us
    pallas_call x1, Pallas kernels, forward(): pl.pallas_call(functools.partial(forward_kernel, chips), out_shape=(shape...  17.2 us
    ppermute x8, waiting for transfers between devices, swap(): return lax.ppermute(array, 'band', [(0, 1), (1, 0)])  14.3 us
    pallas_call x1, Pallas kernels, attention_back(): pl.pallas_call(functools.partial(attention_back_kernel, chips), out_shape...  13.7 us
    pallas_call x7, Pallas kernels, combine(): pl.pallas_call(functools.partial(combine_kernel, jobs, len(recv_list), le...  11.6 us
  transfers between devices with their start and end apart: 33, of which 14 were waited for; matrix products, arithmetic and copies ran while one was open for 6% of the time, Pallas kernels for 25%

profile of v2, /device:TPU:0, one launch (start us, length us, event | category | flops | bytes accessed | tf_op | source)
XLA Modules:
  0.0 261.9 jit_solution(2042274369073324915)
XLA Ops:
  1.5 2.1 copy-done
  4.7 2.2 pick.3
  6.9 3.0 %collective-permute-start.1 = (bf16[160,768]{1,0:T(8,128)(2,1)S(1)}, bf16[160,768]{1,0:T(8,128)(2,1)S(1)}, u32[]{:S(2)}, u32[]{:S(2)}) collective-permute-start(bf16[160,768]{1,0:T(8,128)(2,1)S(1)} %get-tuple-element.109), channel_id=1, source_target_pairs={{0,1},{1,0},{2,3},{3,2},{4,5},{5,4},{6,7},{7,6},{8,9},{9,8},{10,11... | collective-permute-start | bytes 737288 | tf_op jit(solution)/shard_map/ppermute | solution.py:695
  10.7 1.6 copy-done.32
  12.3 4.9 %act_grad.1.after_ref.gact_ref = bf16[784,3072]{1,0:T(8,128)(2,1)S(1)} custom-call(bf16[784,768]{1,0:T(8,128)(2,1)S(1)} %maximum_maximum_fusion.cot_ref, bf16[3072,768]{1,0:T(8,128)(2,1)S(1)} %copy-done.32), custom_call_target="tpu_custom_call" | custom-call | flops 3699376128 | bytes 10000000 | tf_op jit(solution)/shard_map/act_grad/pallas_call | solution.py:255
  17.2 2.2 copy-done.45
  20.7 1.8 copy.34
  25.4 2.1 copy-done.1
  27.5 2.9 %pick.2 = (bf16[320,768]{1,0:T(8,128)(2,1)S(1)}, bf16[160,768]{1,0:T(8,128)(2,1)}) custom-call(s32[2]{0:T(128)S(1)} %get-tuple-element.212.where_ref, s32[12,1,128]{2,1,0:T(1,128)S(1)} %reshape.250.seen_ref, bf16[24,320,256]{2,1,0:T(8,128)(2,1)S(1)} %bitcast.73, bf16[2,160,768]{2,1,0:T(8,128)(2,1)S(1)} %bitcast.76), custom_call_target="tpu_custom_call" | custom-call | flops 503316480 | bytes 1966080 | tf_op jit(solution)/shard_map/pick/pallas_call | solution.py:66
  32.8 17.2 %encoder_forward.1 = (f32[784,768]{1,0:T(8,128)S(1)}, bf16[784,768]{1,0:T(8,128)(2,1)S(1)}, bf16[784,2304]{1,0:T(8,128)(2,1)S(1)}, bf16[12,6,80,128]{3,2,1,0:T(8...) custom-call(bf16[320,768]{1,0:T(8,128)(2,1)S(1)} %get-tuple-element., ...), custom_call_target="tpu_custom_call" | custom-call | flops 7398752256 | bytes 20000000 | tf_op jit(solution)/shard_map/encoder_forward/pallas_call | solution.py:226
  51.5 1.8 copy-done.52
  55.7 16.1 %mlp_both_ways.2 = (bf16[2,2,2,192,384]{4,3,2,1,0:T(8,128)(2,1)}, bf16[2,2,2,192,384]{4,3,2,1,0:T(8,128)(2,1)S(1)}, bf16[2,2,2,192,384]{4,3,2,1,0:T(8,128)(2,1)}...) custom-call(s32[1]{0:T(128)} %bitcast.core_ref, ...), custom_call_target="tpu_custom_call" | custom-call | flops 11098128384 | bytes 25000000 | tf_op jit(solution)/shard_map/mlp_both_ways/pallas_call | solution.py:336
  73.4 14.9 %mlp_both_ways.3 = (bf16[2,2,2,192,384]{4,3,2,1,0:T(8,128)(2,1)}, bf16[2,2,2,192,384]{4,3,2,1,0:T(8,128)(2,1)S(1)}, bf16[2,2,2,192,384]{4,3,2,1,0:T(8,128)(2,1)}...) custom-call(s32[1]{0:T(128)} %bitcast.core_ref, ...), custom_call_target="tpu_custom_call" | custom-call | flops 11098128384 | bytes 25000000 | tf_op jit(solution)/shard_map/mlp_both_ways/pallas_call | solution.py:336
  94.9 2.1 combine.7
  97.0 2.0 collective-permute-start.6
  99.0 1.5 collective-permute-start.7
  100.6 2.0 copy-done.53
  102.6 1.7 copy-done.57
  104.3 1.7 copy-done.59
  107.2 13.7 %attention_back.1 = (f32[784,768]{1,0:T(8,128)S(1)}, bf16[784,2304]{1,0:T(8,128)(2,1)S(1)}, bf16[2,2,4,48,384]{4,3,2,1,0:T(8,128)(2,1)S(1)}, bf16[2,2,4,48,384]{4,3,2,1,0:T(8,128)(2,1)S(1)}, f32[2,768]{1,0:T(2,128)S(1)}) custom-call(s32[1]{0:T(128)} %bitcast.core_ref, f32[784,768]{1,0:T(8,128)S(1)} %copy-done.59, f32[784,768]{1,0:T(8,128)S(1)} %copy-done.57, ...), custom_call_target="tpu_custom_call" | custom-call | flops 5549064192 | bytes 20000000 | tf_op jit(solution)/shard_map/attention_back/pallas_call | solution.py:485
  121.1 4.0 %combine.8 = (bf16[1152,384]{1,0:T(8,128)(2,1)S(1)}, bf16[1152,384]{1,0:T(8,128)(2,1)S(1)}, bf16[384,384]{1,0:T(8,128)(2,1)S(1)}, bf16[384,384]{1,0:T(8,128)(2,1...) custom-call(s32[5]{0:T(128)S(1)} %stack.57.bits_ref, bf16[768,384]{1,0:T(8,128)(2,1)S(1)} %get-tuple-element.134.refs_0_, ...), custom_call_target="tpu_custom_call" | custom-call | flops 1000000 | bytes 6000000 | tf_op jit(solution)/shard_map/combine/pallas_call | solution.py:807
  126.0 5.6 %qkv_grad.1 = (bf16[2,2,4,48,384]{4,3,2,1,0:T(8,128)(2,1)S(1)}, bf16[2,2,4,48,384]{4,3,2,1,0:T(8,128)(2,1)S(1)}, bf16[2,2,4,48,384]{4,3,2,1,0:T(8,128)(2,1)S(1)}...) custom-call(s32[1]{0:T(128)} %bitcast.core_ref, ...), custom_call_target="tpu_custom_call" | custom-call | flops 2774532096 | bytes 8000000 | tf_op jit(solution)/shard_map/qkv_grad/pallas_call | solution.py:637
  135.3 11.4 %collective-permute-done.11.refs_8_ = bf16[1152,384]{1,0:T(8,128)(2,1)S(1)} collective-permute-done((bf16[1152,384]{1,0:T(8,128)(2,1)S(1)}, bf16[1152,384]{1,0:T(8,128)(2,1)S(1)}, u32[]{:S(2)}, u32[]{:S(2)}) %collective-permute-start.11) | collective-permute-done | bytes 884768 | tf_op jit(solution)/shard_map/ppermute | solution.py:697
  148.1 1.6 collective-permute-start.16
  150.0 2.0 copy-done.47
  152.0 1.7 copy-done.51
  153.7 10.0 %embed_back.1 = (bf16[672,384]{1,0:T(8,128)(2,1)S(1)}, bf16[640,384]{1,0:T(8,128)(2,1)S(1)}, f32[16,384]{1,0:T(8,128)S(1)}, bf16[320,768]{1,0:T(8,128)(2,1)S(1)}, bf16[320,768]{1,0:T(8,128)(2,1)}) custom-call(s32[5]{0:T(128)S(1)} %stack.57.bits_ref, bf16[784,2304]{1,0:T(8,128)(2,1)S(1)} %copy-done.47, bf16[768,2304]{1,0:T(8,128)(2,1)S(1)} %copy-done.34, ...), custom_call_target="tpu_custom_call" | custom-call | flops 4624220160 | bytes 15000000 | tf_op jit(solution)/shard_map/embed_back/pallas_call | solution.py:596
  164.3 1.5 collective-permute-start.18
  166.0 2.5 collective-permute-done.16.refs_12_
  168.7 7.9 %collective-permute-done.18.refs_10_ = bf16[576,384]{1,0:T(8,128)(2,1)S(1)} collective-permute-done((bf16[576,384]{1,0:T(8,128)(2,1)S(1)}, bf16[576,384]{1,0:T(8,128)(2,1)S(1)}, u32[]{:S(2)}, u32[]{:S(2)}) %collective-permute-start.18) | collective-permute-done | bytes 442400 | tf_op jit(solution)/shard_map/ppermute | solution.py:697
  176.6 2.8 %collective-permute-done.19.refs_11_ = bf16[768,384]{1,0:T(8,128)(2,1)S(1)} collective-permute-done((bf16[768,384]{1,0:T(8,128)(2,1)S(1)}, bf16[768,384]{1,0:T(8,128)(2,1)S(1)}, u32[]{:S(2)}, u32[]{:S(2)}) %collective-permute-start.19) | collective-permute-done | bytes 589856 | tf_op jit(solution)/shard_map/ppermute | solution.py:695
  179.4 1.9 combine.10
  190.0 1.6 collective-permute-start.21
  192.5 2.6 collective-permute-start.23
  195.3 1.5 collective-permute-start.22
  198.2 3.6 %scatter.2.rest_0_ = f32[24,320,256]{2,1,0:T(8,128)} custom-call(s32[1]{0:T(128)} %bitcast.1.base_ref, s32[12,1,128]{2,1,0:T(1,128)S(1)} %reshape.250.seen_ref, bf16[320,768]{1,0:T(8,128)(2,1)S(1)} %copy-done.15), custom_call_target="tpu_custom_call" | custom-call | flops 251658240 | bytes 3932160 | tf_op jit(solution)/shard_map/scatter/pallas_call | solution.py:672
  201.9 11.3 %collective-permute-done.5.grad_ref = bf16[320,768]{1,0:T(8,128)(2,1)S(1)} collective-permute-done((bf16[320,768]{1,0:T(8,128)(2,1)}, bf16[320,768]{1,0:T(8,128)(2,1)S(1)}, u32[]{:S(2)}, u32[]{:S(2)}) %collective-permute-start.5) | collective-permute-done | bytes 491552 | tf_op jit(solution)/shard_map/ppermute | solution.py:695
  213.1 3.6 %scatter.3 = f32[24,320,256]{2,1,0:T(8,128)} custom-call(s32[1]{0:T(128)} %bitcast.5.base_ref, s32[12,1,128]{2,1,0:T(1,128)S(1)} %reshape.250.seen_ref, bf16[320,768]{1,0:T(8,128)(2,1)S(1)} %collective-permute-done.5.grad_ref, f32[24,320,256]{2,1,0:T(8,128)} %scatter.2.rest_0_), custom_call_target="tpu_custom_call", output_to_operand_aliasing={{}: (3, {})} | custom-call | flops 251658240 | bytes 3932160 | tf_op jit(solution)/shard_map/scatter/pallas_call | solution.py:672
  218.1 2.6 %collective-permute-start.32 = (bf16[288,384]{1,0:T(8,128)(2,1)S(1)}, bf16[288,384]{1,0:T(8,128)(2,1)S(1)}, u32[]{:S(2)}, u32[]{:S(2)}) collective-permute-start(bf16[288,384]{1,0:T(8,128)(2,1)S(1)} %get-tuple-element.199), channel_id=1, source_target_pairs={{0,16},{2,18},{4,20},{6,22},{8,24},{10,26},{12,28},{14,30},{16,0},... | collective-permute-start | bytes 663560 | tf_op jit(solution)/shard_map/ppermute | solution.py:697
  222.3 1.6 collective-permute-start.25
  223.9 2.8 %collective-permute-done.24.refs_6_ = bf16[288,384]{1,0:T(8,128)(2,1)S(1)} collective-permute-done((bf16[288,384]{1,0:T(8,128)(2,1)S(1)}, bf16[288,384]{1,0:T(8,128)(2,1)S(1)}, u32[]{:S(2)}, u32[]{:S(2)}) %collective-permute-start.24) | collective-permute-done | bytes 221216 | tf_op jit(solution)/shard_map/ppermute | solution.py:697
  226.7 4.8 %collective-permute-done.25.refs_7_ = bf16[288,384]{1,0:T(8,128)(2,1)S(1)} collective-permute-done((bf16[288,384]{1,0:T(8,128)(2,1)S(1)}, bf16[288,384]{1,0:T(8,128)(2,1)S(1)}, u32[]{:S(2)}, u32[]{:S(2)}) %collective-permute-start.25) | collective-permute-done | bytes 221216 | tf_op jit(solution)/shard_map/ppermute | solution.py:697
  232.1 1.9 collective-permute-start.30
  236.0 2.4 collective-permute-start.26
  238.5 4.6 %collective-permute-done.26.refs_2_ = bf16[192,384]{1,0:T(8,128)(2,1)S(1)} collective-permute-done((bf16[192,384]{1,0:T(8,128)(2,1)S(1)}, bf16[192,384]{1,0:T(8,128)(2,1)S(1)}, u32[]{:S(2)}, u32[]{:S(2)}) %collective-permute-start.26) | collective-permute-done | bytes 147488 | tf_op jit(solution)/shard_map/ppermute | solution.py:697
  245.7 5.7 %collective-permute-done.27 = bf16[192,384]{1,0:T(8,128)(2,1)S(1)} collective-permute-done((bf16[192,384]{1,0:T(8,128)(2,1)S(1)}, bf16[192,384]{1,0:T(8,128)(2,1)S(1)}, u32[]{:S(2)}, u32[]{:S(2)}) %collective-permute-start.27) | collective-permute-done | bytes 147488 | tf_op jit(solution)/shard_map/ppermute | solution.py:697
  251.5 4.8 %collective-permute-done.28 = bf16[2,80,384]{2,1,0:T(8,128)(2,1)S(1)} collective-permute-done((bf16[2,80,384]{2,1,0:T(8,128)(2,1)S(1)}, bf16[2,80,384]{2,1,0:T(8,128)(2,1)S(1)}, u32[]{:S(2)}, u32[]{:S(2)}) %collective-permute-start.28) | collective-permute-done | bytes 122912 | tf_op jit(solution)/shard_map/ppermute | solution.py:697
  260.2 1.7 reshape.288
  (244 shorter events, 52.6 us)
Async XLA Ops:
  6.9 15.6 %collective-permute-start.1 = (bf16[160,768]{1,0:T(8,128)(2,1)S(1)}, bf16[160,768]{1,0:T(8,128)(2,1)S(1)}, u32[]{:S(2)}, u32[]{:S(2)}) collective-permute-start(bf16[160,768]{1,0:T(8,128)(2,1)S(1)} %get-tuple-element.109), channel_id=1, source_target_pairs={{0,1},{1,0},{2,3},{3,2},{4,5},{5,4},{6,7},{7,6},{8,9},{9,8},{10,11... | collective-permute-start | bytes 737288 | tf_op jit(solution)/shard_map/ppermute | solution.py:695
  9.9 22.1 %collective-permute-start = (bf16[320,768]{1,0:T(8,128)(2,1)S(1)}, bf16[320,768]{1,0:T(8,128)(2,1)S(1)}, u32[]{:S(2)}, u32[]{:S(2)}) collective-permute-start(bf16[320,768]{1,0:T(8,128)(2,1)S(1)} %get-tuple-element.108), channel_id=1, source_target_pairs={{0,1},{1,0},{2,3},{3,2},{4,5},{5,4},{6,7},{7,6},{8,9},{9,8},{10,11... | collective-permute-start | bytes 1474568 | tf_op jit(solution)/shard_map/ppermute | solution.py:695
  22.5 8.0 %collective-permute-start.2 = (bf16[160,768]{1,0:T(8,128)(2,1)S(1)}, bf16[160,768]{1,0:T(8,128)(2,1)}, u32[]{:S(2)}, u32[]{:S(2)}) collective-permute-start(bf16[160,768]{1,0:T(8,128)(2,1)S(1)} %collective-permute-done.1), channel_id=1, source_target_pairs={{0,2},{2,0},{4,6},{6,4},{8,10},{10,8},{12,14},{14,12},{16,18},{18,... | collective-permute-start | bytes 737288 | tf_op jit(solution)/shard_map/ppermute | solution.py:697
  32.0 18.1 %copy-start.37 = (bf16[320,768]{1,0:T(8,128)(2,1)}, bf16[320,768]{1,0:T(8,128)(2,1)S(1)}, u32[]{:S(2)}) copy-start(bf16[320,768]{1,0:T(8,128)(2,1)S(1)} %collective-permute-done.xr_ref) | copy-start | bytes 1474564
  32.0 23.7 %slice-start = ((s8[4718592]{0:T(1024)(128)(4,1)}), s8[4194304]{0:T(1024)(128)(4,1)S(1)}, s32[]{:S(2)}) async-start(s8[4718592]{0:T(1024)(128)(4,1)} %bitcast.87), calls=%async_computation | async-start | bytes 8388608
  32.8 22.9 %slice-start.1 = ((s8[4718592]{0:T(1024)(128)(4,1)}), s8[524288]{0:T(1024)(128)(4,1)S(1)}, s32[]{:S(2)}) async-start(s8[4718592]{0:T(1024)(128)(4,1)} %bitcast.87), calls=%async_computation.1 | async-start | bytes 1048576
  55.5 16.3 %copy-start.56 = (f32[784,768]{1,0:T(8,128)}, f32[784,768]{1,0:T(8,128)S(1)}, u32[]{:S(2)}) copy-start(f32[784,768]{1,0:T(8,128)S(1)} %get-tuple-element.111.out_in_ref.mid_ref) | copy-start | bytes 7225348
  55.5 16.3 %copy-start.62 = (bf16[784,768]{1,0:T(8,128)(2,1)}, bf16[784,768]{1,0:T(8,128)(2,1)S(1)}, u32[]{:S(2)}) copy-start(bf16[784,768]{1,0:T(8,128)(2,1)S(1)} %get-tuple-element.116.att_ref) | copy-start | bytes 3612676
  55.5 16.3 %copy-start.64 = (bf16[12,80,16]{2,1,0:T(8,128)(2,1)}, bf16[12,80,16]{2,1,0:T(8,128)(2,1)S(1)}, u32[]{:S(2)}) copy-start(bf16[12,80,16]{2,1,0:T(8,128)(2,1)S(1)} %get-tuple-element.119.tprobs_ref) | copy-start | bytes 92164
  72.9 15.4 %copy-start.12 = (bf16[2,2,2,192,384]{4,3,2,1,0:T(8,128)(2,1)}, bf16[2,2,2,192,384]{4,3,2,1,0:T(8,128)(2,1)S(1)}, u32[]{:S(2)}) copy-start(bf16[2,2,2,192,384]{4,3,2,1,0:T(8,128)(2,1)S(1)} %get-tuple-element.121) | copy-start | bytes 3538948
  72.9 19.5 %collective-permute-start.3 = (bf16[1536,384]{1,0:T(8,128)(2,1)}, bf16[1536,384]{1,0:T(8,128)(2,1)}, u32[]{:S(2)}, u32[]{:S(2)}) collective-permute-start(bf16[1536,384]{1,0:T(8,128)(2,1)} %bitcast.24), channel_id=1, source_target_pairs={{0,2},{2,0},{4,6},{6,4},{8,10},{10,8},{12,14},{14,12},{16,18},{18,... | collective-permute-start | bytes 3538952 | tf_op jit(solution)/shard_map/ppermute | solution.py:697
  73.2 19.1 %collective-permute-start.4 = (bf16[1536,384]{1,0:T(8,128)(2,1)}, bf16[1536,384]{1,0:T(8,128)(2,1)}, u32[]{:S(2)}, u32[]{:S(2)}) collective-permute-start(bf16[1536,384]{1,0:T(8,128)(2,1)} %bitcast.25), channel_id=1, source_target_pairs={{0,2},{2,0},{4,6},{6,4},{8,10},{10,8},{12,14},{14,12},{16,18},{18,... | collective-permute-start | bytes 3538952 | tf_op jit(solution)/shard_map/ppermute | solution.py:697
  91.8 29.3 %collective-permute-start.8 = (bf16[1536,384]{1,0:T(8,128)(2,1)}, bf16[1536,384]{1,0:T(8,128)(2,1)}, u32[]{:S(2)}, u32[]{:S(2)}) collective-permute-start(bf16[1536,384]{1,0:T(8,128)(2,1)} %bitcast.30), channel_id=1, source_target_pairs={{0,2},{2,0},{4,6},{6,4},{8,10},{10,8},{12,14},{14,12},{16,18},{18,... | collective-permute-start | bytes 3538952 | tf_op jit(solution)/shard_map/ppermute | solution.py:697
  92.1 28.9 %collective-permute-start.9 = (bf16[1536,384]{1,0:T(8,128)(2,1)}, bf16[1536,384]{1,0:T(8,128)(2,1)}, u32[]{:S(2)}, u32[]{:S(2)}) collective-permute-start(bf16[1536,384]{1,0:T(8,128)(2,1)} %bitcast.31), channel_id=1, source_target_pairs={{0,2},{2,0},{4,6},{6,4},{8,10},{10,8},{12,14},{14,12},{16,18},{18,... | collective-permute-start | bytes 3538952 | tf_op jit(solution)/shard_map/ppermute | solution.py:697
  97.0 24.0 %collective-permute-start.6 = (bf16[768,384]{1,0:T(8,128)(2,1)S(1)}, bf16[768,384]{1,0:T(8,128)(2,1)S(1)}, u32[]{:S(2)}, u32[]{:S(2)}) collective-permute-start(bf16[768,384]{1,0:T(8,128)(2,1)S(1)} %get-tuple-element.124.rest_0_), channel_id=1, source_target_pairs={{0,4},{2,6},{4,0},{6,2},{8,12},{10,14},{12,8},{14,10},{16,20},{18,... | collective-permute-start | bytes 1769480 | tf_op jit(solution)/shard_map/ppermute | solution.py:697
  99.0 22.0 %collective-permute-start.7 = (bf16[768,384]{1,0:T(8,128)(2,1)S(1)}, bf16[768,384]{1,0:T(8,128)(2,1)S(1)}, u32[]{:S(2)}, u32[]{:S(2)}) collective-permute-start(bf16[768,384]{1,0:T(8,128)(2,1)S(1)} %get-tuple-element.125.rest_1_), channel_id=1, source_target_pairs={{0,1},{1,0},{2,3},{3,2},{4,5},{5,4},{6,7},{7,6},{8,9},{9,8},{10,11... | collective-permute-start | bytes 1769480 | tf_op jit(solution)/shard_map/ppermute | solution.py:695
  121.0 11.2 %collective-permute-start.12 = (bf16[768,384]{1,0:T(8,128)(2,1)S(1)}, bf16[768,384]{1,0:T(8,128)(2,1)S(1)}, u32[]{:S(2)}, u32[]{:S(2)}) collective-permute-start(bf16[768,384]{1,0:T(8,128)(2,1)S(1)} %bitcast.89), channel_id=1, source_target_pairs={{0,2},{2,0},{4,6},{6,4},{8,10},{10,8},{12,14},{14,12},{16,18},{18,... | collective-permute-start | bytes 1769480 | tf_op jit(solution)/shard_map/ppermute | solution.py:697
  125.2 21.5 %collective-permute-start.11 = (bf16[1152,384]{1,0:T(8,128)(2,1)S(1)}, bf16[1152,384]{1,0:T(8,128)(2,1)S(1)}, u32[]{:S(2)}, u32[]{:S(2)}) collective-permute-start(bf16[1152,384]{1,0:T(8,128)(2,1)S(1)} %get-tuple-element.146.rest_1_), channel_id=1, source_target_pairs={{0,4},{2,6},{4,0},{6,2},{8,12},{10,14},{12,8},{14,10},{16,20},{18,... | collective-permute-start | bytes 2654216 | tf_op jit(solution)/shard_map/ppermute | solution.py:697
  125.8 21.2 %collective-permute-start.10 = (bf16[1152,384]{1,0:T(8,128)(2,1)S(1)}, bf16[1152,384]{1,0:T(8,128)(2,1)S(1)}, u32[]{:S(2)}, u32[]{:S(2)}) collective-permute-start(bf16[1152,384]{1,0:T(8,128)(2,1)S(1)} %get-tuple-element.145.rest_0_), channel_id=1, source_target_pairs={{0,1},{1,0},{2,3},{3,2},{4,5},{5,4},{6,7},{7,6},{8,9},{9,8},{10,11... | collective-permute-start | bytes 2654216 | tf_op jit(solution)/shard_map/ppermute | solution.py:695
  131.5 2.1 collective-permute-start.13
  131.6 2.8 %collective-permute-start.14 = (bf16[768,384]{1,0:T(8,128)(2,1)S(1)}, bf16[768,384]{1,0:T(8,128)(2,1)S(1)}, u32[]{:S(2)}, u32[]{:S(2)}) collective-permute-start(bf16[768,384]{1,0:T(8,128)(2,1)S(1)} %bitcast.91), channel_id=1, source_target_pairs={{0,2},{2,0},{4,6},{6,4},{8,10},{10,8},{12,14},{14,12},{16,18},{18,... | collective-permute-start | bytes 1769480 | tf_op jit(solution)/shard_map/ppermute | solution.py:697
  132.1 3.2 %collective-permute-start.15 = (bf16[768,384]{1,0:T(8,128)(2,1)S(1)}, bf16[768,384]{1,0:T(8,128)(2,1)S(1)}, u32[]{:S(2)}, u32[]{:S(2)}) collective-permute-start(bf16[768,384]{1,0:T(8,128)(2,1)S(1)} %bitcast.90), channel_id=1, source_target_pairs={{0,2},{2,0},{4,6},{6,4},{8,10},{10,8},{12,14},{14,12},{16,18},{18,... | collective-permute-start | bytes 1769480 | tf_op jit(solution)/shard_map/ppermute | solution.py:697
  148.1 20.4 %collective-permute-start.16 = (bf16[1152,384]{1,0:T(8,128)(2,1)S(1)}, bf16[1152,384]{1,0:T(8,128)(2,1)S(1)}, u32[]{:S(2)}, u32[]{:S(2)}) collective-permute-start(bf16[1152,384]{1,0:T(8,128)(2,1)S(1)} %get-tuple-element.158), channel_id=1, source_target_pairs={{0,4},{2,6},{4,0},{6,2},{8,12},{10,14},{12,8},{14,10},{16,20},{18,... | collective-permute-start | bytes 2654216 | tf_op jit(solution)/shard_map/ppermute | solution.py:697
  163.7 5.0 %collective-permute-start.17 = (bf16[672,384]{1,0:T(8,128)(2,1)S(1)}, bf16[672,384]{1,0:T(8,128)(2,1)S(1)}, u32[]{:S(2)}, u32[]{:S(2)}) collective-permute-start(bf16[672,384]{1,0:T(8,128)(2,1)S(1)} %get-tuple-element.163), channel_id=1, source_target_pairs={{0,2},{2,0},{4,6},{6,4},{8,10},{10,8},{12,14},{14,12},{16,18},{18,... | collective-permute-start | bytes 1548296 | tf_op jit(solution)/shard_map/ppermute | solution.py:697
  163.7 15.7 %collective-permute-start.19 = (bf16[768,384]{1,0:T(8,128)(2,1)S(1)}, bf16[768,384]{1,0:T(8,128)(2,1)S(1)}, u32[]{:S(2)}, u32[]{:S(2)}) collective-permute-start(bf16[768,384]{1,0:T(8,128)(2,1)S(1)} %get-tuple-element.165), channel_id=1, source_target_pairs={{0,1},{1,0},{2,3},{3,2},{4,5},{5,4},{6,7},{7,6},{8,9},{9,8},{10,11... | collective-permute-start | bytes 1769480 | tf_op jit(solution)/shard_map/ppermute | solution.py:695
  164.3 12.3 %collective-permute-start.18 = (bf16[576,384]{1,0:T(8,128)(2,1)S(1)}, bf16[576,384]{1,0:T(8,128)(2,1)S(1)}, u32[]{:S(2)}, u32[]{:S(2)}) collective-permute-start(bf16[576,384]{1,0:T(8,128)(2,1)S(1)} %get-tuple-element.164), channel_id=1, source_target_pairs={{0,8},{2,10},{4,12},{6,14},{8,0},{10,2},{12,4},{14,6},{16,24},{18,... | collective-permute-start | bytes 1327112 | tf_op jit(solution)/shard_map/ppermute | solution.py:697
  188.0 28.8 %collective-permute-start.20 = (bf16[736,384]{1,0:T(8,128)(2,1)}, bf16[736,384]{1,0:T(8,128)(2,1)S(1)}, u32[]{:S(2)}, u32[]{:S(2)}) collective-permute-start(bf16[736,384]{1,0:T(8,128)(2,1)} %get-tuple-element.174), channel_id=1, source_target_pairs={{0,1},{1,0},{2,3},{3,2},{4,5},{5,4},{6,7},{7,6},{8,9},{9,8},{10,11... | collective-permute-start | bytes 1695752 | tf_op jit(solution)/shard_map/ppermute | solution.py:695
  188.6 24.5 %collective-permute-start.5 = (bf16[320,768]{1,0:T(8,128)(2,1)}, bf16[320,768]{1,0:T(8,128)(2,1)S(1)}, u32[]{:S(2)}, u32[]{:S(2)}) collective-permute-start(bf16[320,768]{1,0:T(8,128)(2,1)} %get-tuple-element.130), channel_id=1, source_target_pairs={{0,1},{1,0},{2,3},{3,2},{4,5},{5,4},{6,7},{7,6},{8,9},{9,8},{10,11... | collective-permute-start | bytes 1474568 | tf_op jit(solution)/shard_map/ppermute | solution.py:695
  190.0 26.8 %collective-permute-start.21 = (bf16[576,384]{1,0:T(8,128)(2,1)}, bf16[576,384]{1,0:T(8,128)(2,1)}, u32[]{:S(2)}, u32[]{:S(2)}) collective-permute-start(bf16[576,384]{1,0:T(8,128)(2,1)} %get-tuple-element.175), channel_id=1, source_target_pairs={{0,8},{2,10},{4,12},{6,14},{8,0},{10,2},{12,4},{14,6},{16,24},{18,... | collective-permute-start | bytes 1327112 | tf_op jit(solution)/shard_map/ppermute | solution.py:697
  192.5 24.2 %collective-permute-start.23 = (bf16[288,384]{1,0:T(8,128)(2,1)S(1)}, bf16[288,384]{1,0:T(8,128)(2,1)S(1)}, u32[]{:S(2)}, u32[]{:S(2)}) collective-permute-start(bf16[288,384]{1,0:T(8,128)(2,1)S(1)} %copy-done.42), channel_id=1, source_target_pairs={{0,16},{2,18},{4,20},{6,22},{8,24},{10,26},{12,28},{14,30},{16,0},... | collective-permute-start | bytes 663560 | tf_op jit(solution)/shard_map/ppermute | solution.py:697
  195.3 21.5 %collective-permute-start.22 = (bf16[192,384]{1,0:T(8,128)(2,1)S(1)}, bf16[192,384]{1,0:T(8,128)(2,1)S(1)}, u32[]{:S(2)}, u32[]{:S(2)}) collective-permute-start(bf16[192,384]{1,0:T(8,128)(2,1)S(1)} %copy-done.44), channel_id=1, source_target_pairs={{0,4},{2,6},{4,0},{6,2},{8,12},{10,14},{12,8},{14,10},{16,20},{18,... | collective-permute-start | bytes 442376 | tf_op jit(solution)/shard_map/ppermute | solution.py:697
  201.8 15.0 %copy-start.17 = (bf16[384,384]{1,0:T(8,128)(2,1)S(1)}, bf16[384,384]{1,0:T(8,128)(2,1)}, u32[]{:S(2)}) copy-start(bf16[384,384]{1,0:T(8,128)(2,1)} %copy-done.16) | copy-start | bytes 884740
  201.8 15.0 %copy-start.19 = (bf16[320,384]{1,0:T(8,128)(2,1)S(1)}, bf16[320,384]{1,0:T(8,128)(2,1)}, u32[]{:S(2)}) copy-start(bf16[320,384]{1,0:T(8,128)(2,1)} %copy-done.18) | copy-start | bytes 737284
  201.8 15.0 %copy-start.21 = (bf16[192,384]{1,0:T(8,128)(2,1)S(1)}, bf16[192,384]{1,0:T(8,128)(2,1)}, u32[]{:S(2)}) copy-start(bf16[192,384]{1,0:T(8,128)(2,1)} %copy-done.20) | copy-start | bytes 442372
  201.8 15.0 %copy-start.23 = (bf16[192,384]{1,0:T(8,128)(2,1)S(1)}, bf16[192,384]{1,0:T(8,128)(2,1)}, u32[]{:S(2)}) copy-start(bf16[192,384]{1,0:T(8,128)(2,1)} %copy-done.22) | copy-start | bytes 442372
  201.8 15.0 %copy-start.25 = (bf16[192,384]{1,0:T(8,128)(2,1)S(1)}, bf16[192,384]{1,0:T(8,128)(2,1)}, u32[]{:S(2)}) copy-start(bf16[192,384]{1,0:T(8,128)(2,1)} %copy-done.24) | copy-start | bytes 442372
  201.8 15.0 %copy-start.27 = (bf16[192,384]{1,0:T(8,128)(2,1)S(1)}, bf16[192,384]{1,0:T(8,128)(2,1)}, u32[]{:S(2)}) copy-start(bf16[192,384]{1,0:T(8,128)(2,1)} %copy-done.26) | copy-start | bytes 442372
  201.8 15.0 %copy-start.29 = (bf16[192,384]{1,0:T(8,128)(2,1)S(1)}, bf16[192,384]{1,0:T(8,128)(2,1)}, u32[]{:S(2)}) copy-start(bf16[192,384]{1,0:T(8,128)(2,1)} %copy-done.28) | copy-start | bytes 442372
  201.8 15.0 %copy-start.31 = (f32[16,384]{1,0:T(8,128)S(1)}, f32[16,384]{1,0:T(8,128)}, u32[]{:S(2)}) copy-start(f32[16,384]{1,0:T(8,128)} %copy-done.30) | copy-start | bytes 73732
  218.1 16.4 %collective-permute-start.32 = (bf16[288,384]{1,0:T(8,128)(2,1)S(1)}, bf16[288,384]{1,0:T(8,128)(2,1)S(1)}, u32[]{:S(2)}, u32[]{:S(2)}) collective-permute-start(bf16[288,384]{1,0:T(8,128)(2,1)S(1)} %get-tuple-element.199), channel_id=1, source_target_pairs={{0,16},{2,18},{4,20},{6,22},{8,24},{10,26},{12,28},{14,30},{16,0},... | collective-permute-start | bytes 663560 | tf_op jit(solution)/shard_map/ppermute | solution.py:697
  220.8 5.9 %collective-permute-start.24 = (bf16[288,384]{1,0:T(8,128)(2,1)S(1)}, bf16[288,384]{1,0:T(8,128)(2,1)S(1)}, u32[]{:S(2)}, u32[]{:S(2)}) collective-permute-start(bf16[288,384]{1,0:T(8,128)(2,1)S(1)} %get-tuple-element.184), channel_id=1, source_target_pairs={{0,4},{2,6},{4,0},{6,2},{8,12},{10,14},{12,8},{14,10},{16,20},{18,... | collective-permute-start | bytes 663560 | tf_op jit(solution)/shard_map/ppermute | solution.py:697
  222.3 9.2 %collective-permute-start.25 = (bf16[288,384]{1,0:T(8,128)(2,1)S(1)}, bf16[288,384]{1,0:T(8,128)(2,1)S(1)}, u32[]{:S(2)}, u32[]{:S(2)}) collective-permute-start(bf16[288,384]{1,0:T(8,128)(2,1)S(1)} %get-tuple-element.185), channel_id=1, source_target_pairs={{0,8},{2,10},{4,12},{6,14},{8,0},{10,2},{12,4},{14,6},{16,24},{18,... | collective-permute-start | bytes 663560 | tf_op jit(solution)/shard_map/ppermute | solution.py:697
  232.1 12.2 %collective-permute-start.30 = (bf16[144,384]{1,0:T(8,128)(2,1)S(1)}, bf16[144,384]{1,0:T(8,128)(2,1)S(1)}, u32[]{:S(2)}, u32[]{:S(2)}) collective-permute-start(bf16[144,384]{1,0:T(8,128)(2,1)S(1)} %get-tuple-element.193), channel_id=1, source_target_pairs={{0,16},{2,18},{4,20},{6,22},{8,24},{10,26},{12,28},{14,30},{16,0},... | collective-permute-start | bytes 331784 | tf_op jit(solution)/shard_map/ppermute | solution.py:697
  234.0 4.5 %collective-permute-start.31 = (bf16[48,384]{1,0:T(8,128)(2,1)S(1)}, bf16[48,384]{1,0:T(8,128)(2,1)S(1)}, u32[]{:S(2)}, u32[]{:S(2)}) collective-permute-start(bf16[48,384]{1,0:T(8,128)(2,1)S(1)} %get-tuple-element.196), channel_id=1, source_target_pairs={{0,1},{1,0},{2,3},{3,2},{4,5},{5,4},{6,7},{7,6},{8,9},{9,8},{10,11... | collective-permute-start | bytes 110600 | tf_op jit(solution)/shard_map/ppermute | solution.py:695
  236.0 7.1 %collective-permute-start.26 = (bf16[192,384]{1,0:T(8,128)(2,1)S(1)}, bf16[192,384]{1,0:T(8,128)(2,1)S(1)}, u32[]{:S(2)}, u32[]{:S(2)}) collective-permute-start(bf16[192,384]{1,0:T(8,128)(2,1)S(1)} %get-tuple-element.188), channel_id=1, source_target_pairs={{0,8},{2,10},{4,12},{6,14},{8,0},{10,2},{12,4},{14,6},{16,24},{18,... | collective-permute-start | bytes 442376 | tf_op jit(solution)/shard_map/ppermute | solution.py:697
  243.7 7.7 %collective-permute-start.27 = (bf16[192,384]{1,0:T(8,128)(2,1)S(1)}, bf16[192,384]{1,0:T(8,128)(2,1)S(1)}, u32[]{:S(2)}, u32[]{:S(2)}) collective-permute-start(bf16[192,384]{1,0:T(8,128)(2,1)S(1)} %get-tuple-element.190), channel_id=1, source_target_pairs={{0,16},{2,18},{4,20},{6,22},{8,24},{10,26},{12,28},{14,30},{16,0},... | collective-permute-start | bytes 442376 | tf_op jit(solution)/shard_map/ppermute | solution.py:697
  251.4 4.9 %collective-permute-start.28 = (bf16[2,80,384]{2,1,0:T(8,128)(2,1)S(1)}, bf16[2,80,384]{2,1,0:T(8,128)(2,1)S(1)}, u32[]{:S(2)}, u32[]{:S(2)}) collective-permute-start(bf16[2,80,384]{2,1,0:T(8,128)(2,1)S(1)} %bitcast.102), channel_id=1, source_target_pairs={{0,4},{2,6},{4,0},{6,2},{8,12},{10,14},{12,8},{14,10},{16,20},{18,... | collective-permute-start | bytes 368648 | tf_op jit(solution)/shard_map/ppermute | solution.py:697
  256.4 3.1 %collective-permute-start.29 = (bf16[2,2,80,384]{3,2,1,0:T(8,128)(2,1)S(1)}, bf16[2,2,80,384]{3,2,1,0:T(8,128)(2,1)S(1)}, u32[]{:S(2)}, u32[]{:S(2)}) collective-permute-start(bf16[2,2,80,384]{3,2,1,0:T(8,128)(2,1)S(1)} %maximum_select_fusion.3), channel_id=1, source_target_pairs={{0,2},{2,0},{4,6},{6,4},{8,10},{10,8},{12,14},{14,12},{16,18},{18,... | collective-permute-start | bytes 737288 | tf_op jit(solution)/shard_map/ppermute | solution.py:697
  (62 other events, 160.0 us)
